TPU v7x, 256 devices: a whole 4x4x8 slice. The times are simulated.
256 devices in a mesh: seq: 32 (over z, x), grp: 8 (over y, core).
Axes of the slice: x: 4, y: 4, z: 8, core: 2. Of those that a mesh axis runs over, the one named last changes fastest.
Arguments:
- queries: bfloat16 [8, 4096, 2048], P('grp', 'seq'), may hold values from -500 to 500
- grad_out: bfloat16 [8, 4096, 2048], P('grp', 'seq'), may hold values from -6 to 6
- enc_states: bfloat16 [8, 256, 128, 512], P('grp', 'seq'), may hold values from -6 to 6
- neighbour_ids: int32 [8, 64, 2], P('grp', 'seq'), may hold values from 0 to 255, as said below
- kv_weight: bfloat16 [2, 512, 2048], replicated, may hold values from -0.25 to 0.25
Outputs:
- grad_queries: bfloat16 [8, 4096, 2048], P('grp', 'seq')
- grad_states: bfloat16 [8, 256, 128, 512], P('grp', 'seq')
- grad_weight: float32 [2, 512, 2048], P(None, 'seq', 'grp')
Inputs may be any that keep to these rules, and one draw needn't show every extreme that they name: `neighbour_ids`: block b is held at position b % 8 by the device of index b // 8 along seq. Of the 4 references of one device's spans, at most 1 name blocks held by any one device, and that many do so for some device.
All inputs are finite; a program needn't handle non-finite values.
Results may differ from a plain program's by a relative error of at most 0.012.
The roundings to bfloat16 on the way count: a program that leaves them out, or rounds other values in their place, can miss the bound.
Values may be sent and summed in bfloat16 or wider, within the bound.
A program may use at most 128 MiB of HBM per device.

v0:
```python
import math

import jax
import jax.numpy as jnp
from jax import lax
from jax.sharding import PartitionSpec as P

DH = 128


def body(queries, grad_out, enc_states, neighbour_ids, kv_weight):
    bf16 = jnp.bfloat16
    f32 = jnp.float32
    seq_count = lax.axis_size("seq")
    tok_rows = queries.shape[1]
    head_width = queries.shape[2]
    span_count = neighbour_ids.shape[1]
    nbr_count = neighbour_ids.shape[2]
    span_len = tok_rows // span_count
    blocks_dev = enc_states.shape[1]
    nbr_len = enc_states.shape[2]
    enc_width = enc_states.shape[3]
    head_count = head_width // DH
    flat_refs = neighbour_ids.reshape(-1)
    ref_count = flat_refs.shape[0]
    slot_cap = -(-ref_count // seq_count)
    owners = flat_refs // blocks_dev
    local_slot = flat_refs % blocks_dev
    ref_order = jnp.arange(ref_count)
    same_owner = (owners[:, None] == owners[None, :]) & (ref_order[None, :] < ref_order[:, None])
    position = jnp.sum(same_owner.astype(jnp.int32), axis=1)
    slot_index = owners * slot_cap + position
    placing = slot_index[:, None] == jnp.arange(seq_count * slot_cap)[None, :]
    wanted = jnp.sum(jnp.where(placing, local_slot[:, None] + 1, 0), axis=0) - 1
    asked = lax.all_to_all(
        wanted.reshape(seq_count, slot_cap), "seq", split_axis=0, concat_axis=0, tiled=True
    )
    picking = (asked[:, :, None] == jnp.arange(blocks_dev)[None, None, :]).astype(bf16)
    replies = jnp.einsum(
        "sab,btc->satc", picking, enc_states[0], preferred_element_type=f32
    ).astype(bf16)
    arrived = lax.all_to_all(replies, "seq", split_axis=0, concat_axis=0, tiled=True)
    placing_b = placing.astype(bf16)
    states = jnp.einsum(
        "rs,stc->rtc",
        placing_b,
        arrived.reshape(seq_count * slot_cap, nbr_len, enc_width),
        preferred_element_type=f32,
    ).astype(bf16)
    flat_states = states.reshape(ref_count * nbr_len, enc_width)
    key_rows = jnp.dot(flat_states, kv_weight[0], preferred_element_type=f32).astype(bf16)
    value_rows = jnp.dot(flat_states, kv_weight[1], preferred_element_type=f32).astype(bf16)
    key_h = key_rows.reshape(span_count, nbr_count * nbr_len, head_count, DH)
    value_h = value_rows.reshape(span_count, nbr_count * nbr_len, head_count, DH)
    query_h = queries[0].reshape(span_count, span_len, head_count, DH)
    grad_h = grad_out[0].reshape(span_count, span_len, head_count, DH)
    score_scale = 1.0 / math.sqrt(DH)
    scores = jnp.einsum("cqhd,ckhd->chqk", query_h, key_h, preferred_element_type=f32) * score_scale
    top_score = jnp.max(scores, axis=-1, keepdims=True)
    expo = jnp.exp(scores - top_score)
    weights_f = expo / jnp.sum(expo, axis=-1, keepdims=True)
    weights_b = weights_f.astype(bf16)
    attended = jnp.einsum("chqk,ckhd->cqhd", weights_b, value_h, preferred_element_type=f32)
    row_delta = jnp.sum(grad_h.astype(f32) * attended, axis=-1)
    grad_v = jnp.einsum("chqk,cqhd->ckhd", weights_b, grad_h, preferred_element_type=f32).astype(
        bf16
    )
    grad_p = jnp.einsum("cqhd,ckhd->chqk", grad_h, value_h, preferred_element_type=f32)
    grad_s = (
        weights_f * (grad_p - jnp.swapaxes(row_delta, 1, 2)[:, :, :, None]) * score_scale
    ).astype(bf16)
    grad_q = jnp.einsum("chqk,ckhd->cqhd", grad_s, key_h, preferred_element_type=f32).astype(bf16)
    grad_k = jnp.einsum("chqk,cqhd->ckhd", grad_s, query_h, preferred_element_type=f32).astype(bf16)
    grad_queries = grad_q.reshape(1, tok_rows, head_width)
    flat_k = grad_k.reshape(ref_count * nbr_len, head_width)
    flat_v = grad_v.reshape(ref_count * nbr_len, head_width)
    back_dims = (((1,), (1,)), ((), ()))
    grad_e = lax.dot_general(flat_k, kv_weight[0], back_dims, preferred_element_type=f32)
    grad_e = (
        grad_e + lax.dot_general(flat_v, kv_weight[1], back_dims, preferred_element_type=f32)
    ).astype(bf16)
    grad_e = grad_e.reshape(ref_count, nbr_len, enc_width)
    sending = jnp.einsum("rs,rtc->stc", placing_b, grad_e, preferred_element_type=f32).astype(bf16)
    sending = sending.reshape(seq_count, slot_cap, nbr_len, enc_width)
    summed = jnp.einsum(
        "sab,satc->btc",
        picking,
        lax.all_to_all(sending, "seq", split_axis=0, concat_axis=0, tiled=True),
        preferred_element_type=f32,
    )
    grad_states = summed.astype(bf16)[None]
    row_dims = (((0,), (0,)), ((), ()))
    partial_grad = jnp.stack(
        [
            lax.dot_general(flat_states, flat_k, row_dims, preferred_element_type=f32),
            lax.dot_general(flat_states, flat_v, row_dims, preferred_element_type=f32),
        ]
    )
    row_share = lax.psum_scatter(partial_grad, "seq", scatter_dimension=1, tiled=True)
    grad_weight = lax.psum_scatter(row_share, "grp", scatter_dimension=2, tiled=True)
    return (grad_queries, grad_states, grad_weight)


def solution(mesh):
    placed = (
        P("grp", "seq", None),
        P("grp", "seq", None),
        P("grp", "seq", None, None),
        P("grp", "seq", None),
        P(),
    )
    return jax.shard_map(
        body,
        mesh=mesh,
        in_specs=placed,
        out_specs=(P("grp", "seq", None), P("grp", "seq", None, None), P(None, "seq", "grp")),
        check_vma=False,
    )
```

profile of v0, /device:TPU:1, one launch (start us, length us, event | category | flops | bytes accessed | tf_op | source)
XLA Modules:
  0.0 487.2 jit_solution(15513754221228831053)
XLA Ops:
  7.2 0.0 copy-start
  7.2 0.8 reshape.211
  8.0 0.2 convert_reduce_fusion
  8.2 0.1 select_reduce_fusion
  8.3 0.1 copy.75
  8.4 20.2 %all_to_all.19 = s32[32,1,1]{2,1,0:T(1,128)S(1)} all-to-all(s32[32,1,1]{2,1,0:T(1,128)S(1)} %copy.75), channel_id=1, replica_groups=mesh['seq'=32,'grp'=8] {'seq'}, dimensions={0} | all-to-all | bytes 256 | tf_op jit(solution)/shard_map/all_to_all | solution.py:35
  28.7 0.7 reduce
  29.3 0.0 copy-done
  29.3 1.3 convert_bitcast_fusion.1
  30.6 4.4 copy.77
  35.0 5.0 %all-to-all-start.1 = ((bf16[32,1,128,512]{3,2,1,0:T(8,128)(2,1)}), bf16[32,1,128,512]{3,2,1,0:T(8,128)(2,1)}, u32[]{:S(2)}, u32[]{:S(2)}) async-start(bf16[32,1,128,512]{3,2,1,0:T(8,128)(2,1)} %copy.77), calls=%async_computation.1 | async-start | bytes 8388608 | tf_op jit(solution)/shard_map/all_to_all | solution.py:42
  40.0 0.2 reduce-scatter.3.cloned.1.call-start
  40.2 0.0 copy-done.10
  40.2 0.1 copy.97
  40.3 0.0 copy-done.11
  40.4 0.9 copy.99
  41.3 91.5 %all-to-all-done.1 = bf16[32,1,128,512]{3,2,1,0:T(8,128)(2,1)} async-done(((bf16[32,1,128,512]{3,2,1,0:T(8,128)(2,1)}), bf16[32,1,128,512]{3,2,1,0:T(8,128)(2,1)}, u32[]{:S(2)}, u32[]{:S(2)}) %all-to-all-start.1) | async-done | bytes 4194336 | tf_op jit(solution)/shard_map/all_to_all | solution.py:42
  132.7 4.8 fusion.68
  137.5 0.1 copy.79
  137.6 0.0 copy-start.12
  137.6 0.0 copy-done.15
  137.6 1.3 fusion.43
  138.9 0.0 copy-done.12
  138.9 1.3 fusion.40
  140.2 2.0 copy.98
  142.1 0.6 copy.96
  142.8 0.9 fusion.28
  143.6 0.0 copy-start.2
  143.6 0.0 copy-start.14
  143.6 1.8 fusion.113
  145.4 0.2 copy-done.2
  145.7 7.9 %convert_bitcast_fusion.2 = bf16[2,256,16,128]{3,1,2,0:T(8,128)(2,1)} fusion(bf16[2,64,16,128]{3,2,1,0:T(8,128)(2,1)S(1)} %bitcast.161, f32[2,16,64]{2,1,0:T(8,128)S(1)} %get-tuple-element.20, f32[2,16,256,64]{2,3,1,0:T(8,128)} %copy-done.2), kind=kOutput, calls=%fused_computation.31 | convolution fusion | flops 137890048 | bytes 4726784 | tf_op jit(solution)/shard_map/chqk,cqhd->ckhd/dot_general | solution.py:65
  153.5 6.8 %fusion.76 = f32[2,64,16]{1,2,0:T(8,128)S(1)} fusion(bf16[2,256,16,128]{3,2,1,0:T(8,128)(2,1)} %bitcast.152, bf16[2,64,16,128]{3,2,1,0:T(8,128)(2,1)S(1)} %bitcast.162, f32[2,16,64]{2,1,0:T(8,128)S(1)} %get-tuple-element.20, f32[2,16,256,64]{2,3,1,0:T(8,128)} %copy-done.2), kind=kOutput, calls=%fused_computation.60 | convolution fusion | flops 137625856 | bytes 4734976 | tf_op jit(solution)/shard_map/chqk,ckhd->cqhd/dot_general | solution.py:63
  160.3 0.0 copy-start.8
  160.3 0.0 copy-start.9
  160.3 3.3 copy.91
  163.7 0.0 copy-start.5
  163.7 0.0 copy-done.8
  163.7 0.0 copy-done.9
  163.7 1.2 fusion.14
  164.9 0.0 copy-start.3
  164.9 0.8 convert_bitcast_fusion.3
  165.7 1.4 copy.89
  167.1 1.3 convolution_bitcast_fusion.1
  168.4 1.3 convolution_bitcast_fusion
  169.7 3.8 pad_maximum_fusion
  173.5 0.0 reduce-scatter.3.cloned.1.call-update
  173.5 0.0 copy-start.16
  173.5 3.7 fusion.8
  177.2 0.4 copy-done.16
  177.6 1.3 fusion.71
  178.9 1.4 convert_bitcast_fusion
  180.3 4.4 copy.93
  184.6 6.9 %all-to-all-start.2 = ((bf16[32,1,128,512]{3,2,1,0:T(8,128)(2,1)}), bf16[32,1,128,512]{3,2,1,0:T(8,128)(2,1)}, u32[]{:S(2)}, u32[]{:S(2)}) async-start(bf16[32,1,128,512]{3,2,1,0:T(8,128)(2,1)} %copy.93), calls=%async_computation.2 | async-start | bytes 8388608 | tf_op jit(solution)/shard_map/all_to_all | solution.py:88
  191.6 0.0 reduce-scatter.5.cloned.1.call-start
  191.6 252.4 %reduce-scatter.3.cloned.1.call-done = f32[2,16,2048]{2,1,0:T(8,128)} async-done(((f32[2,512,2048]{2,1,0:T(8,128)}), f32[2,16,2048]{2,1,0:T(8,128)}) %reduce-scatter.3.cloned.1.call-update) | async-done | bytes 262160 | tf_op jit(solution)/shard_map/reduce_scatter | solution.py:99
  444.0 0.0 reduce-scatter.5.cloned.1.call-update
  444.0 0.7 fusion.79
  444.8 0.3 copy.87
  445.1 1.0 reshape.216
  446.1 0.0 all-to-all-done.2
  446.2 4.6 fusion.51
  450.8 1.3 copy.95
  452.1 28.3 %reduce-scatter.5.cloned.1.call-done = f32[2,16,256]{2,1,0:T(8,128)} async-done(((f32[2,16,2048]{2,1,0:T(8,128)}), f32[2,16,256]{2,1,0:T(8,128)}) %reduce-scatter.5.cloned.1.call-update) | async-done | bytes 32784 | tf_op jit(solution)/shard_map/reduce_scatter | solution.py:100
  (19 shorter events, 0.1 us)
Async XLA Ops:
  7.2 22.2 %copy-start = (bf16[1,8,128,512]{3,2,1,0:T(8,128)(2,1)S(1)}, bf16[1,8,128,512]{3,2,1,0:T(8,128)(2,1)}, u32[]{:S(2)}) copy-start(bf16[1,8,128,512]{3,2,1,0:T(8,128)(2,1)} %param.7) | copy-start | bytes 3145732
  35.0 5.2 %copy-start.10 = (bf16[1,128,2048]{2,1,0:T(8,128)(2,1)S(1)}, bf16[1,128,2048]{2,1,0:T(8,128)(2,1)}, u32[]{:S(2)}) copy-start(bf16[1,128,2048]{2,1,0:T(8,128)(2,1)} %param.5) | copy-start | bytes 1572868
  35.0 5.4 %copy-start.11 = (bf16[1,128,2048]{2,1,0:T(8,128)(2,1)S(1)}, bf16[1,128,2048]{2,1,0:T(8,128)(2,1)}, u32[]{:S(2)}) copy-start(bf16[1,128,2048]{2,1,0:T(8,128)(2,1)} %param.6) | copy-start | bytes 1572868
  35.0 97.7 %all-to-all-start.1 = ((bf16[32,1,128,512]{3,2,1,0:T(8,128)(2,1)}), bf16[32,1,128,512]{3,2,1,0:T(8,128)(2,1)}, u32[]{:S(2)}, u32[]{:S(2)}) async-start(bf16[32,1,128,512]{3,2,1,0:T(8,128)(2,1)} %copy.77), calls=%async_computation.1 | async-start | bytes 8388608 | tf_op jit(solution)/shard_map/all_to_all | solution.py:42
  40.0 404.0 %reduce-scatter.3.cloned.1.call-start = ((), (), s32[]{:S(2)}) async-start(), calls=%async_computation.5 | async-start | bytes 8650752 | tf_op jit(solution)/shard_map/reduce_scatter | solution.py:99
  132.7 4.9 %copy-start.15 = (bf16[2,512,2048]{2,1,0:T(8,128)(2,1)S(1)}, bf16[2,512,2048]{2,1,0:T(8,128)(2,1)}, u32[]{:S(2)}) copy-start(bf16[2,512,2048]{2,1,0:T(8,128)(2,1)} %param.9) | copy-start | bytes 12582916
  137.6 1.3 copy-start.12
  143.6 2.0 copy-start.2
  143.6 2.0 copy-start.14
  160.3 3.3 copy-start.8
  160.3 3.3 copy-start.9
  163.7 4.7 copy-start.5
  164.9 2.1 copy-start.3
  165.7 1.4 copy-start.13
  167.0 1.3 copy-start.6
  173.5 3.7 copy-start.7
  173.5 4.1 copy-start.16
  184.6 259.4 %copy-start.4 = (bf16[2,16,64,256]{3,2,1,0:T(8,128)(2,1)S(1)}, bf16[2,16,64,256]{3,2,1,0:T(8,128)(2,1)}, u32[]{:S(2)}) copy-start(bf16[2,16,64,256]{3,2,1,0:T(8,128)(2,1)} %copy-done.3) | copy-start | bytes 3145732
  184.6 261.5 %all-to-all-start.2 = ((bf16[32,1,128,512]{3,2,1,0:T(8,128)(2,1)}), bf16[32,1,128,512]{3,2,1,0:T(8,128)(2,1)}, u32[]{:S(2)}, u32[]{:S(2)}) async-start(bf16[32,1,128,512]{3,2,1,0:T(8,128)(2,1)} %copy.93), calls=%async_computation.2 | async-start | bytes 8388608 | tf_op jit(solution)/shard_map/all_to_all | solution.py:88
  191.6 288.8 %reduce-scatter.5.cloned.1.call-start = ((), (), s32[]{:S(2)}) async-start(), calls=%async_computation.6 | async-start | bytes 294912 | tf_op jit(solution)/shard_map/reduce_scatter | solution.py:100
  446.2 34.2 %copy-start.1 = (bf16[1,8,128,512]{3,2,1,0:T(8,128)(2,1)S(1)}, bf16[1,8,128,512]{3,2,1,0:T(8,128)(2,1)}, u32[]{:S(2)}) copy-start(bf16[1,8,128,512]{3,2,1,0:T(8,128)(2,1)} %param.7) | copy-start | bytes 3145732
Sparse Core Ops, SparseCore 0:
  173.6 270.3 reduce-scatter.2
  447.2 33.0 reduce-scatter.4
where the time goes:
time: 489 us; the launch traced here: 487 us
  waiting for transfers between devices  372 us (76%)
  matrix products  40.4 us (8%)
  local copies, waits for them, and re-layouts  21.3 us (4%)
  blocking collectives  20.2 us (4%)
  between operations  14.4 us (3%)
  starting transfers between devices  12.2 us (2%)
  other arithmetic  6.54 us (1%)
    reduce_scatter x1, waiting for transfers between devices, body(): lax.psum_scatter(partial_grad, 'seq', scatter_dimension=1, tiled=True)  252 us
    all_to_all x1, waiting for transfers between devices, body(): lax.all_to_all(replies, 'seq', split_axis=0, concat_axis=0, tiled=True)  91.5 us
    reduce_scatter x1, waiting for transfers between devices, body(): lax.psum_scatter(row_share, 'grp', scatter_dimension=2, tiled=True)  28.3 us
    all_to_all x1, blocking collectives, body(): lax.all_to_all(wanted.reshape(seq_count, slot_cap), 'seq', split_axis=0,...  20.2 us
  transfers between devices with their start and end apart: 4, of which 3 were waited for; matrix products, arithmetic and copies ran while one was open for 4% of the time, Pallas kernels for 0%

commit v1 on v0

v1 whole, which is shorter than its diff:
```python
import functools
import math

import jax
import jax.numpy as jnp
from jax import lax
from jax.experimental import pallas as pl
from jax.experimental.pallas import tpu as pltpu
from jax.sharding import PartitionSpec as P

DH = 128
BF = jnp.bfloat16
F32 = jnp.float32
MESH = pl.DeviceIdType.MESH
NT = (((1,), (1,)), ((), ()))
TN = (((0,), (0,)), ((), ()))


def attention_kernel(states_ref, w_ref, q_ref, go_ref, gq_ref, ge_ref, dw_ref, st_ref, acc_ref):
    step = pl.program_id(0)
    scale = 1.0 / math.sqrt(DH)

    @pl.when(step == 0)
    def _():
        st_ref[...] = states_ref[...].T
        acc_ref[...] = jnp.zeros_like(acc_ref)

    states = states_ref[...]
    wk = w_ref[0]
    wv = w_ref[1]
    keys = jnp.dot(states, wk, preferred_element_type=F32).astype(BF)
    values = jnp.dot(states, wv, preferred_element_type=F32).astype(BF)
    blank = jnp.zeros((64, DH), BF)
    gk_parts = []
    gv_parts = []
    for span in range(2):
        q = q_ref[span * 64 : span * 64 + 64, :]
        go = go_ref[span * 64 : span * 64 + 64, :]
        key = keys[span * 256 : span * 256 + 256, :]
        value = values[span * 256 : span * 256 + 256, :]
        qd = jnp.concatenate(
            [
                jnp.concatenate([q[:, :DH], blank], axis=1),
                jnp.concatenate([blank, q[:, DH:]], axis=1),
            ],
            axis=0,
        )
        gd = jnp.concatenate(
            [
                jnp.concatenate([go[:, :DH], blank], axis=1),
                jnp.concatenate([blank, go[:, DH:]], axis=1),
            ],
            axis=0,
        )
        scores = lax.dot_general(key, qd, NT, preferred_element_type=F32) * scale
        top = jnp.max(scores, axis=0, keepdims=True)
        expo = jnp.exp(scores - top)
        weights = expo / jnp.sum(expo, axis=0, keepdims=True)
        weights_b = weights.astype(BF)
        gp = lax.dot_general(value, gd, NT, preferred_element_type=F32)
        delta = jnp.sum(weights_b.astype(F32) * gp, axis=0, keepdims=True)
        gs = (weights * (gp - delta) * scale).astype(BF)
        gv_parts.append(jnp.dot(weights_b, gd, preferred_element_type=F32).astype(BF))
        gk_parts.append(jnp.dot(gs, qd, preferred_element_type=F32).astype(BF))
        gq = lax.dot_general(gs, key, TN, preferred_element_type=F32).astype(BF)
        gq_ref[span * 64 : span * 64 + 64, :DH] = gq[:64, :DH]
        gq_ref[span * 64 : span * 64 + 64, DH:] = gq[64:, DH:]
    gk = jnp.concatenate(gk_parts, axis=0)
    gv = jnp.concatenate(gv_parts, axis=0)
    total = acc_ref[...]
    total = total + lax.dot_general(gk, wk, NT, preferred_element_type=F32)
    total = total + lax.dot_general(gv, wv, NT, preferred_element_type=F32)
    acc_ref[...] = total

    @pl.when(step == pl.num_programs(0) - 1)
    def _():
        ge_ref[...] = total.astype(BF)

    turned = st_ref[...]
    for kind, part in enumerate((gk, gv)):
        share = jnp.dot(turned, part, preferred_element_type=F32).astype(BF)
        for z in range(8):
            for x in range(4):
                row = (z * 4 + x) * 16
                dw_ref[0, x, kind, z] = share[row : row + 16, :]


def attention(states, weights, queries, grad_out):
    keys, enc = states.shape
    tokens, width = queries.shape
    return pl.pallas_call(
        attention_kernel,
        grid=(8,),
        in_specs=[
            pl.BlockSpec((keys, enc), lambda i: (0, 0)),
            pl.BlockSpec((2, enc, 256), lambda i: (0, 0, i)),
            pl.BlockSpec((tokens, 256), lambda i: (0, i)),
            pl.BlockSpec((tokens, 256), lambda i: (0, i)),
        ],
        out_specs=[
            pl.BlockSpec((tokens, 256), lambda i: (0, i)),
            pl.BlockSpec((keys, enc), lambda i: (0, 0)),
            pl.BlockSpec((1, 4, 2, 8, 16, 256), lambda i: (i, 0, 0, 0, 0, 0)),
        ],
        out_shape=[
            jax.ShapeDtypeStruct((tokens, width), BF),
            jax.ShapeDtypeStruct((keys, enc), BF),
            jax.ShapeDtypeStruct((8, 4, 2, 8, 16, 256), BF),
        ],
        scratch_shapes=[pltpu.VMEM((enc, keys), BF), pltpu.VMEM((keys, enc), F32)],
        compiler_params=pltpu.CompilerParams(vmem_limit_bytes=40 * 2**20),
        cost_estimate=pl.CostEstimate(
            flops=7_200_000_000, bytes_accessed=12_000_000, transcendentals=600_000
        ),
    )(states, weights, queries, grad_out)


def reduce_kernel(
    dw_ref, out_ref, pair_in, held, y_half, y_in, x_half, x_in, z_in, core_sem, y_sem, x_sem, z_sem
):
    seq = lax.axis_index("seq")
    grp = lax.axis_index("grp")
    z = seq // 4
    x = seq % 4
    y = grp // 2
    core = grp % 2

    def at(zz, xx, yy, cc):
        return {
            "seq": (zz + 8) % 8 * 4 + (xx + 4) % 4,
            "grp": (yy + 4) % 4 * 2 + cc,
        }

    barrier = pltpu.get_barrier_semaphore()
    friends = [at(z, x, y, 1 - core)]
    friends += [at(z, x, y + step, core) for step in (1, 3)]
    friends += [at(z, x + step, y, core) for step in (1, 3)]
    friends += [at(z + step, x, y, core) for step in range(1, 8)]
    for friend in friends:
        pl.semaphore_signal(barrier, inc=1, device_id=friend, device_id_type=MESH)
    pl.semaphore_wait(barrier, len(friends))

    def send(src, dst, sems, slot, target):
        copy = pltpu.make_async_remote_copy(
            src_ref=src,
            dst_ref=dst,
            send_sem=sems.at[0, slot],
            recv_sem=sems.at[1, slot],
            device_id=target,
            device_id_type=MESH,
        )
        copy.start()
        return copy

    offsets = (2, 1, 3, 0)
    swaps = []
    for slot, offset in enumerate(offsets):
        theirs = (y + offset) % 4 * 2 + 1 - core
        swaps.append(
            send(dw_ref.at[theirs], pair_in.at[slot], core_sem, slot, at(z, x, y, 1 - core))
        )

    def add_pair(slot, offset):
        swaps[slot].wait_recv()
        mine = (y + offset) % 4 * 2 + core
        for part in range(4):
            held[slot, part] = (
                dw_ref[mine, part].astype(F32) + pair_in[slot, part].astype(F32)
            ).astype(BF)

    add_pair(0, 2)
    up = send(held.at[0, pl.ds(0, 2)], y_half.at[0], y_sem, 0, at(z, x, y + 1, core))
    down = send(held.at[0, pl.ds(2, 2)], y_half.at[1], y_sem, 1, at(z, x, y - 1, core))
    add_pair(1, 1)
    add_pair(2, 3)
    add_pair(3, 0)
    up.wait_recv()
    for part in range(2):
        held[1, part] = (held[1, part].astype(F32) + y_half[0, part].astype(F32)).astype(BF)
    up2 = send(held.at[1], y_in.at[0], y_sem, 2, at(z, x, y + 1, core))
    down.wait_recv()
    for part in range(2):
        held[2, part + 2] = (
            held[2, part + 2].astype(F32) + y_half[1, part].astype(F32)
        ).astype(BF)
    down2 = send(held.at[2], y_in.at[1], y_sem, 3, at(z, x, y - 1, core))
    up2.wait_recv()
    down2.wait_recv()

    def y_total(offset):
        part = (x + offset) % 4
        return (
            held[3, part].astype(F32)
            + y_in[0, part].astype(F32)
            + y_in[1, part].astype(F32)
        )

    held[4, 0] = y_total(2).astype(BF)
    xup = send(held.at[4, 0, 0], x_half.at[0], x_sem, 0, at(z, x + 1, y, core))
    xdown = send(held.at[4, 0, 1], x_half.at[1], x_sem, 1, at(z, x - 1, y, core))
    ahead = y_total(1)
    behind = y_total(3)
    own = y_total(0)
    xup.wait_recv()
    held[4, 1, 0] = (ahead[0] + x_half[0].astype(F32)).astype(BF)
    held[4, 1, 1] = ahead[1].astype(BF)
    xup2 = send(held.at[4, 1], x_in.at[0], x_sem, 2, at(z, x + 1, y, core))
    xdown.wait_recv()
    held[4, 2, 0] = behind[0].astype(BF)
    held[4, 2, 1] = (behind[1] + x_half[1].astype(F32)).astype(BF)
    xdown2 = send(held.at[4, 2], x_in.at[1], x_sem, 3, at(z, x - 1, y, core))
    xup2.wait_recv()
    xdown2.wait_recv()
    held[4, 3] = (own + x_in[0].astype(F32) + x_in[1].astype(F32)).astype(BF)

    zs = []
    for step in (4, 3, 5, 2, 6, 1, 7):
        target = (z + step) % 8
        zs.append(
            send(
                held.at[4, 3, :, target], z_in.at[step - 1], z_sem, step - 1, at(z + step, x, y, core)
            )
        )
    result = held[4, 3, :, z].astype(F32)
    for copy, step in zip(zs, (4, 3, 5, 2, 6, 1, 7)):
        copy.wait_recv()
        result = result + z_in[step - 1].astype(F32)
    out_ref[...] = result
    for copy in swaps + [up, down, up2, down2, xup, xdown, xup2, xdown2] + zs:
        copy.wait_send()


def reduce_weights(dw):
    return pl.pallas_call(
        reduce_kernel,
        in_specs=[pl.BlockSpec(memory_space=pltpu.VMEM)],
        out_specs=pl.BlockSpec(memory_space=pltpu.VMEM),
        out_shape=jax.ShapeDtypeStruct((2, 16, 256), F32),
        scratch_shapes=[
            pltpu.VMEM((4, 4, 2, 8, 16, 256), BF),
            pltpu.VMEM((5, 4, 2, 8, 16, 256), BF),
            pltpu.VMEM((2, 2, 2, 8, 16, 256), BF),
            pltpu.VMEM((2, 4, 2, 8, 16, 256), BF),
            pltpu.VMEM((2, 8, 16, 256), BF),
            pltpu.VMEM((2, 2, 8, 16, 256), BF),
            pltpu.VMEM((7, 2, 16, 256), BF),
            pltpu.SemaphoreType.DMA((2, 4)),
            pltpu.SemaphoreType.DMA((2, 4)),
            pltpu.SemaphoreType.DMA((2, 4)),
            pltpu.SemaphoreType.DMA((2, 7)),
        ],
        compiler_params=pltpu.CompilerParams(
            collective_id=1, has_side_effects=True, vmem_limit_bytes=40 * 2**20
        ),
    )(dw)


def body(queries, grad_out, enc_states, neighbour_ids, kv_weight):
    seq_count = lax.axis_size("seq")
    blocks_dev = enc_states.shape[1]
    nbr_len = enc_states.shape[2]
    enc_width = enc_states.shape[3]
    flat_refs = neighbour_ids.reshape(-1)
    ref_count = flat_refs.shape[0]
    owners = flat_refs // blocks_dev
    local_slot = flat_refs % blocks_dev
    placing = owners[:, None] == jnp.arange(seq_count)[None, :]
    wanted = jnp.sum(jnp.where(placing, local_slot[:, None] + 1, 0), axis=0) - 1
    asked = lax.all_to_all(
        wanted.reshape(seq_count, 1), "seq", split_axis=0, concat_axis=0, tiled=True
    ).reshape(-1)
    replies = jnp.take(enc_states[0], jnp.maximum(asked, 0), axis=0)
    arrived = lax.all_to_all(replies, "seq", split_axis=0, concat_axis=0, tiled=True)
    states = jnp.take(arrived, owners, axis=0)
    flat_states = states.reshape(ref_count * nbr_len, enc_width)
    gq, grad_e, dw = attention(flat_states, kv_weight, queries[0], grad_out[0])
    grad_weight = reduce_weights(dw)
    placing_b = placing.astype(BF)
    grad_e = grad_e.reshape(ref_count, nbr_len, enc_width)
    sending = jnp.einsum("rs,rtc->stc", placing_b, grad_e, preferred_element_type=F32).astype(BF)
    picking = (asked[:, None] == jnp.arange(blocks_dev)[None, :]).astype(BF)
    summed = jnp.einsum(
        "sb,stc->btc",
        picking,
        lax.all_to_all(sending, "seq", split_axis=0, concat_axis=0, tiled=True),
        preferred_element_type=F32,
    )
    grad_states = summed.astype(BF)[None]
    return (gq[None], grad_states, grad_weight)


def solution(mesh):
    placed = (
        P("grp", "seq", None),
        P("grp", "seq", None),
        P("grp", "seq", None, None),
        P("grp", "seq", None),
        P(),
    )
    return jax.shard_map(
        body,
        mesh=mesh,
        in_specs=placed,
        out_specs=(P("grp", "seq", None), P("grp", "seq", None, None), P(None, "seq", "grp")),
        check_vma=False,
    )
```

time: 489 us -> 269 us (0.55)
  waiting for transfers between devices: 372 us -> 92.5 us
  Pallas kernels: 0 us -> 107 us
  matrix products: 40.4 us -> 5.93 us
  between operations: 14.4 us -> 0.77 us
    reduce_scatter x2 -> x0, waiting for transfers between devices: 281 us -> none  [the longest x1 252 us: body(): lax.psum_scatter(partial_grad, 'seq', scatter_dimension=1, tiled=True)]
    pallas_call x0 -> x2, Pallas kernels: none -> 107 us  [the longest x1 89.6 us: reduce_weights(): pl.pallas_call(reduce_kernel, in_specs=[pl.BlockSpec(memory_space=pltpu.V...]
    dot_general x16 -> x2, matrix products: 40.4 us -> 5.93 us  [the longest x1 4.55 us: body(): jnp.einsum('sb,stc->btc', picking, lax.all_to_all(sending, 'seq', split_a...]
    gather x0 -> x2, local copies, waits for them, and re-layouts: none -> 5.56 us  [the longest x1 2.79 us: body(): replies = jnp.take(enc_states[0], jnp.maximum(asked, 0), axis=0)]
    reshape x2 -> x0, local copies, waits for them, and re-layouts: 5.37 us -> none  [the longest x1 4.35 us: body(): sending = sending.reshape(seq_count, slot_cap, nbr_len, enc_width)]
    convert_element_type x5 -> x1, local copies, waits for them, and re-layouts: 9.47 us -> 4.37 us  [body(): jnp.einsum('rs,rtc->stc', placing_b, grad_e, preferred_element_type=F32)]
  transfers between devices with their start and end apart: 4 -> 2, of which waited for: 3 -> 1; matrix products, arithmetic and copies ran while one was open for 4% -> 0% of each run, Pallas kernels for 0% -> 34%
where the time goes in v1:
time: 269 us; the launch traced here: 264 us
  Pallas kernels  107 us (40%)
  waiting for transfers between devices  92.5 us (34%)
  blocking collectives  20.2 us (8%)
  local copies, waits for them, and re-layouts  19.3 us (7%)
  starting transfers between devices  12 us (4%)
  other arithmetic  6.15 us (2%)
  matrix products  5.93 us (2%)
    all_to_all x1, waiting for transfers between devices, body(): lax.all_to_all(replies, 'seq', split_axis=0, concat_axis=0, tiled=True)  92.5 us
    pallas_call x1, Pallas kernels, reduce_weights(): pl.pallas_call(reduce_kernel, in_specs=[pl.BlockSpec(memory_space=pltpu.V...  89.6 us
    all_to_all x1, blocking collectives, body(): lax.all_to_all(wanted.reshape(seq_count, 1), 'seq', split_axis=0, concat_...  20.2 us
    pallas_call x1, Pallas kernels, attention(): pl.pallas_call(attention_kernel, grid=(8,), in_specs=[pl.BlockSpec((keys,...  17.1 us
    unnamed x16, local copies, waits for them, and re-layouts  8.24 us
    all_to_all x1, starting transfers between devices, body(): lax.all_to_all(sending, 'seq', split_axis=0, concat_axis=0, tiled=True)  6.98 us
  transfers between devices with their start and end apart: 2, of which 1 were waited for; matrix products, arithmetic and copies ran while one was open for 0% of the time, Pallas kernels for 34%

profile of v1, /device:TPU:1, one launch (start us, length us, event | category | flops | bytes accessed | tf_op | source)
XLA Modules:
  0.0 263.5 jit_solution(5214624011465869629)
XLA Ops:
  0.6 0.0 copy-start
  0.6 0.8 reshape.165
  1.5 0.1 select_reduce_fusion
  1.6 0.1 copy.12
  1.7 20.2 %all_to_all.19 = s32[32,1,1]{2,1,0:T(1,128)S(1)} all-to-all(s32[32,1,1]{2,1,0:T(1,128)S(1)} %copy.12), channel_id=1, replica_groups=mesh['seq'=32,'grp'=8] {'seq'}, dimensions={0} | all-to-all | bytes 256 | tf_op jit(solution)/shard_map/all_to_all | solution.py:269
  21.9 1.2 fusion.17
  23.2 0.0 copy-done
  23.2 2.8 %gather_fusion = bf16[32,128,512]{2,1,0:T(8,128)(2,1)} fusion(bf16[8,128,512]{2,1,0:T(8,128)(2,1)S(1)} %bitcast.21, s32[1024]{0:T(1024)S(1)} %pad_clamp_fusion.1), kind=kCustom, calls=%fused_computation | custom fusion | bytes 8388736 | tf_op jit(solution)/shard_map/jit(_take)/gather | solution.py:272
  26.0 4.6 %broadcast_select_fusion = bf16[32,128,512]{2,1,0:T(8,128)(2,1)} fusion(bf16[32,128,512]{2,1,0:T(8,128)(2,1)} %gather_fusion, pred[32]{0:T(512)(128)(4,1)S(1)} %maximum_compare_fusion), kind=kLoop, calls=%fused_computation.4 | loop fusion | flops 2097152 | bytes 8388640 | tf_op jit(solution)/shard_map/jit(_take)/select_n | solution.py:272
  30.6 0.0 copy-start.6
  30.6 0.0 copy-start.4
  30.6 0.0 copy-start.5
  30.6 5.0 %all-to-all-start.1 = ((bf16[32,128,512]{2,1,0:T(8,128)(2,1)}), bf16[32,128,512]{2,1,0:T(8,128)(2,1)}, u32[]{:S(2)}, u32[]{:S(2)}) async-start(bf16[32,128,512]{2,1,0:T(8,128)(2,1)} %broadcast_select_fusion), calls=%async_computation.1 | async-start | bytes 8388608 | tf_op jit(solution)/shard_map/all_to_all | solution.py:273
  35.6 0.0 copy-done.6
  35.6 0.1 reshape.166
  35.8 0.1 broadcast_bitcast_fusion
  35.8 92.5 %all-to-all-done.1 = bf16[32,128,512]{2,1,0:T(8,128)(2,1)} async-done(((bf16[32,128,512]{2,1,0:T(8,128)(2,1)}), bf16[32,128,512]{2,1,0:T(8,128)(2,1)}, u32[]{:S(2)}, u32[]{:S(2)}) %all-to-all-start.1) | async-done | bytes 4194336 | tf_op jit(solution)/shard_map/all_to_all | solution.py:273
  128.4 2.8 %gather_fusion.1 = bf16[4,128,512]{2,1,0:T(8,128)(2,1)S(1)} fusion(bf16[32,128,512]{2,1,0:T(8,128)(2,1)} %all-to-all-done.1, s32[1024]{0:T(1024)S(1)} %pad_clamp_fusion), kind=kCustom, calls=%fused_computation.1 | custom fusion | bytes 1048592 | tf_op jit(solution)/shard_map/jit(_take)/gather | solution.py:274
  131.1 0.1 bitcast_select_fusion.states_ref
  131.3 0.0 copy-done.4
  131.3 0.0 copy-done.5
  131.3 0.0 copy-start.3
  131.3 2.2 copy-done.3
  133.5 17.1 %shard_map.76 = (bf16[128,2048]{1,0:T(8,128)(2,1)}, bf16[512,512]{1,0:T(8,128)(2,1)S(1)}, bf16[8,4,2,8,16,256]{5,4,3,2,1,0:T(8,128)(2,1)S(1)}) custom-call(bf16[512,512]{1,0:T(8,128)(2,1)S(1)} %bitcast_select_fusion.states_ref, bf16[2,512,2048]{2,1,0:T(8,128)(2,1)S(1)} %copy-done.3, bf16[128,2048]{1,0:T(8,128)(2,1)S(1)} %bitcast.23, ...), custom_call_target="tpu_custom_call" | custom-call | flops 7200000000 | bytes 12000000 | tf_op jit(solution)/shard_map/pallas_call | solution.py:91
  150.6 0.0 copy-start.1
  150.6 2.0 copy-done.1
  152.5 1.4 convolution_convert_fusion
  153.9 4.4 %copy.14 = bf16[32,128,512]{2,1,0:T(8,128)(2,1)} copy(bf16[32,128,512]{2,0,1:T(8,128)(2,1)S(1)} %convolution_convert_fusion) | data formatting | bytes 8388608 | tf_op jit(solution)/shard_map/convert_element_type | solution.py:280
  158.3 7.0 %all-to-all-start.2 = ((bf16[32,128,512]{2,1,0:T(8,128)(2,1)}), bf16[32,128,512]{2,1,0:T(8,128)(2,1)}, u32[]{:S(2)}, u32[]{:S(2)}) async-start(bf16[32,128,512]{2,1,0:T(8,128)(2,1)} %copy.14), calls=%async_computation.2 | async-start | bytes 8388608 | tf_op jit(solution)/shard_map/all_to_all | solution.py:285
  165.3 0.0 copy-start.2
  165.3 2.2 copy-done.2
  167.5 89.6 %shard_map.77 = f32[2,16,256]{2,1,0:T(8,128)S(1)} custom-call(bf16[8,4,2,8,16,256]{5,4,3,2,1,0:T(8,128)(2,1)S(1)} %copy-done.2), custom_call_target="tpu_custom_call" | custom-call | tf_op jit(solution)/shard_map/pallas_call | solution.py:234
  257.1 0.0 all-to-all-done.2
  257.1 4.5 %fusion.5 = bf16[1,8,128,512]{3,1,2,0:T(8,128)(2,1)S(1)} fusion(bf16[32,128,512]{2,1,0:T(8,128)(2,1)} %all-to-all-done.2, s32[32]{0:T(128)S(1)} %get-tuple-element.18), kind=kOutput, calls=%fused_computation.7 | convolution fusion | flops 34078976 | bytes 5243008 | tf_op jit(solution)/shard_map/sb,stc->btc/dot_general | solution.py:282
  261.6 1.3 copy.16
  262.9 0.6 copy.26
  (7 shorter events, 0.1 us)
Async XLA Ops:
  0.6 22.6 %copy-start = (bf16[1,8,128,512]{3,2,1,0:T(8,128)(2,1)S(1)}, bf16[1,8,128,512]{3,2,1,0:T(8,128)(2,1)}, u32[]{:S(2)}) copy-start(bf16[1,8,128,512]{3,2,1,0:T(8,128)(2,1)} %param.7) | copy-start | bytes 3145732
  30.6 5.0 %copy-start.6 = (s32[1,2,2]{2,1,0:T(2,128)S(1)}, s32[1,2,2]{2,1,0:T(2,128)}, u32[]{:S(2)}) copy-start(s32[1,2,2]{2,1,0:T(2,128)} %param.8) | copy-start | bytes 52
  30.6 100.6 %copy-start.4 = (bf16[1,128,2048]{2,1,0:T(8,128)(2,1)S(1)}, bf16[1,128,2048]{2,1,0:T(8,128)(2,1)}, u32[]{:S(2)}) copy-start(bf16[1,128,2048]{2,1,0:T(8,128)(2,1)} %param.5) | copy-start | bytes 1572868
  30.6 100.7 %copy-start.5 = (bf16[1,128,2048]{2,1,0:T(8,128)(2,1)S(1)}, bf16[1,128,2048]{2,1,0:T(8,128)(2,1)}, u32[]{:S(2)}) copy-start(bf16[1,128,2048]{2,1,0:T(8,128)(2,1)} %param.6) | copy-start | bytes 1572868
  30.6 97.7 %all-to-all-start.1 = ((bf16[32,128,512]{2,1,0:T(8,128)(2,1)}), bf16[32,128,512]{2,1,0:T(8,128)(2,1)}, u32[]{:S(2)}, u32[]{:S(2)}) async-start(bf16[32,128,512]{2,1,0:T(8,128)(2,1)} %broadcast_select_fusion), calls=%async_computation.1 | async-start | bytes 8388608 | tf_op jit(solution)/shard_map/all_to_all | solution.py:273
  131.3 2.2 copy-start.3
  150.6 2.0 copy-start.1
  158.3 98.8 %all-to-all-start.2 = ((bf16[32,128,512]{2,1,0:T(8,128)(2,1)}), bf16[32,128,512]{2,1,0:T(8,128)(2,1)}, u32[]{:S(2)}, u32[]{:S(2)}) async-start(bf16[32,128,512]{2,1,0:T(8,128)(2,1)} %copy.14), calls=%async_computation.2 | async-start | bytes 8388608 | tf_op jit(solution)/shard_map/all_to_all | solution.py:285
  165.3 2.2 copy-start.2

commit v2 on v1

--- a/solution.py
+++ b/solution.py
@@ -115,50 +115,352 @@
     )(states, weights, queries, grad_out)
 
 
-def reduce_kernel(
-    dw_ref, out_ref, pair_in, held, y_half, y_in, x_half, x_in, z_in, core_sem, y_sem, x_sem, z_sem
-):
+def place():
     seq = lax.axis_index("seq")
     grp = lax.axis_index("grp")
-    z = seq // 4
-    x = seq % 4
-    y = grp // 2
-    core = grp % 2
-
-    def at(zz, xx, yy, cc):
-        return {
-            "seq": (zz + 8) % 8 * 4 + (xx + 4) % 4,
-            "grp": (yy + 4) % 4 * 2 + cc,
-        }
-
+    return seq // 4, seq % 4, grp // 2, grp % 2
+
+
+def at(z, x, y, core):
+    return {"seq": (z + 8) % 8 * 4 + (x + 4) % 4, "grp": (y + 4) % 4 * 2 + core}
+
+
+def teammate(z, y, member):
+    return at(z, member // 2, y, member % 2)
+
+
+def greet(friends):
     barrier = pltpu.get_barrier_semaphore()
-    friends = [at(z, x, y, 1 - core)]
-    friends += [at(z, x, y + step, core) for step in (1, 3)]
-    friends += [at(z, x + step, y, core) for step in (1, 3)]
-    friends += [at(z + step, x, y, core) for step in range(1, 8)]
     for friend in friends:
         pl.semaphore_signal(barrier, inc=1, device_id=friend, device_id_type=MESH)
     pl.semaphore_wait(barrier, len(friends))
 
+
+def push(src, dst, send_sem, recv_sem, target):
+    copy = pltpu.make_async_remote_copy(
+        src_ref=src,
+        dst_ref=dst,
+        send_sem=send_sem,
+        recv_sem=recv_sem,
+        device_id=target,
+        device_id_type=MESH,
+    )
+    copy.start()
+    return copy
+
+
+def spread_kernel(row_ref, enc_ref, pool_ref, ids_ref, team_sem, row_sem, z_sem, y_sem, own_sem):
+    z, x, y, core = place()
+    me = x * 2 + core
+    friends = [teammate(z, y, (me + k) % 8) for k in range(1, 8)]
+    friends += [at(z + k, x, y, core) for k in range(1, 8)]
+    friends += [at(z, x, y + k, core) for k in range(1, 4)]
+    ids_ref[y, z, me] = row_ref[...]
+    greet(friends)
+    rows = []
+    for k in range(1, 8):
+        rows.append(
+            push(
+                ids_ref.at[y, z, me],
+                ids_ref.at[y, z, me],
+                row_sem.at[0, k - 1],
+                row_sem.at[1, k - 1],
+                friends[k - 1],
+            )
+        )
+    pieces = []
+    for k in range(1, 8):
+        member = (me + k) % 8
+        pieces.append(
+            push(
+                enc_ref.at[:, pl.ds(pl.multiple_of(member * 16, 16), 16), :],
+                pool_ref.at[me],
+                team_sem.at[0, k - 1],
+                team_sem.at[1, k - 1],
+                friends[k - 1],
+            )
+        )
+    own = pltpu.make_async_copy(
+        enc_ref.at[:, pl.ds(pl.multiple_of(me * 16, 16), 16), :], pool_ref.at[me], own_sem
+    )
+    own.start()
+    for copy in rows:
+        copy.wait_recv()
+    planes = []
+    for k in range(1, 8):
+        planes.append(
+            push(
+                ids_ref.at[y, z],
+                ids_ref.at[y, z],
+                z_sem.at[0, k - 1],
+                z_sem.at[1, k - 1],
+                friends[6 + k],
+            )
+        )
+    for copy in planes:
+        copy.wait_recv()
+    columns = []
+    for k in range(1, 4):
+        columns.append(
+            push(
+                ids_ref.at[y],
+                ids_ref.at[y],
+                y_sem.at[0, k - 1],
+                y_sem.at[1, k - 1],
+                friends[13 + k],
+            )
+        )
+    own.wait()
+    for copy in columns + pieces:
+        copy.wait_recv()
+    for copy in rows + pieces + planes + columns:
+        copy.wait_send()
+
+
+def spread(row, enc):
+    return pl.pallas_call(
+        spread_kernel,
+        in_specs=[
+            pl.BlockSpec(memory_space=pltpu.VMEM),
+            pl.BlockSpec(memory_space=pl.ANY),
+        ],
+        out_specs=[
+            pl.BlockSpec(memory_space=pltpu.VMEM),
+            pl.BlockSpec(memory_space=pltpu.VMEM),
+        ],
+        out_shape=[
+            jax.ShapeDtypeStruct((8, 8, 16, 512), BF),
+            jax.ShapeDtypeStruct((4, 8, 8, 1, 128), jnp.int32),
+        ],
+        scratch_shapes=[
+            pltpu.SemaphoreType.DMA((2, 7)),
+            pltpu.SemaphoreType.DMA((2, 7)),
+            pltpu.SemaphoreType.DMA((2, 7)),
+            pltpu.SemaphoreType.DMA((2, 3)),
+            pltpu.SemaphoreType.DMA,
+        ],
+        compiler_params=pltpu.CompilerParams(
+            collective_id=1, has_side_effects=True, vmem_limit_bytes=16 * 2**20
+        ),
+    )(row, enc)
+
+
+def starts(caps):
+    return [0] + [sum(caps[: r + 1]) for r in range(len(caps))]
+
+
+def gather_kernel(
+    caps, chunk, order_ref, loc_ref, pool_ref, states_ref, packed, arr, stage, ring_sem, team_sem
+):
+    z, x, y, core = place()
+    me = x * 2 + core
+    total = sum(caps)
+    first = starts(caps)
+    friends = [teammate(z, y, (me + k) % 8) for k in range(1, 8)]
+    ahead = at(z + 1, x, y, core)
+    behind = at(z - 1, x, y, core)
+    greet(friends + [ahead, behind])
+    copies = {}
+
+    def forward(d, r, i, src):
+        slot = first[r] + i * chunk
+        index = slot // chunk
+        copies[d, r, i] = push(
+            src,
+            arr.at[pl.ds(d * total + slot, chunk)],
+            ring_sem.at[0, d, index],
+            ring_sem.at[1, d, index],
+            ahead if d == 0 else behind,
+        )
+
+    for i in range(caps[0] // chunk):
+        for d in range(2):
+
+            def fill(j, carry, i=i, d=d):
+                packed[d, i * chunk + j] = pool_ref[order_ref[d, i * chunk + j]]
+                return carry
+
+            lax.fori_loop(0, chunk, fill, 0)
+            forward(d, 0, i, packed.at[d, pl.ds(i * chunk, chunk)])
+
+    def keep(j, carry):
+        arr[2 * total + j] = pool_ref[j]
+        return carry
+
+    lax.fori_loop(0, 64, keep, 0)
+    for r in range(1, 4):
+        for i in range(caps[r] // chunk):
+            for d in range(2):
+                copies[d, r - 1, i].wait_recv()
+                slot = d * total + first[r - 1] + i * chunk
+                forward(d, r, i, arr.at[pl.ds(slot, chunk)])
+    for r in range(4):
+        low = caps[r + 1] // chunk if r < 3 else 0
+        for i in range(low, caps[r] // chunk):
+            for d in range(2):
+                copies[d, r, i].wait_recv()
+
+    def pick(i, carry):
+        for k in range(4):
+            stage[i, k] = arr[loc_ref[i * 4 + k]]
+        return carry
+
+    lax.fori_loop(0, 8, pick, 0)
+    rows = pl.ds(pl.multiple_of(me * 16, 16), 16)
+    hands = []
+    for k in range(1, 8):
+        hands.append(
+            push(
+                stage.at[(me + k) % 8],
+                states_ref.at[:, rows, :],
+                team_sem.at[0, k - 1],
+                team_sem.at[1, k - 1],
+                friends[k - 1],
+            )
+        )
+    states_ref[:, rows, :] = stage[me]
+    for copy in hands:
+        copy.wait_recv()
+    for copy in hands + list(copies.values()):
+        copy.wait_send()
+
+
+def gather(caps, chunk, number, order, loc, pool):
+    total = sum(caps)
+    return pl.pallas_call(
+        functools.partial(gather_kernel, caps, chunk),
+        in_specs=[
+            pl.BlockSpec(memory_space=pltpu.SMEM),
+            pl.BlockSpec(memory_space=pltpu.SMEM),
+            pl.BlockSpec(memory_space=pltpu.VMEM),
+        ],
+        out_specs=pl.BlockSpec(memory_space=pltpu.VMEM),
+        out_shape=jax.ShapeDtypeStruct((4, 128, 512), BF),
+        scratch_shapes=[
+            pltpu.VMEM((2, caps[0], 16, 512), BF),
+            pltpu.VMEM((2 * total + 64, 16, 512), BF),
+            pltpu.VMEM((8, 4, 16, 512), BF),
+            pltpu.SemaphoreType.DMA((2, 2, total // chunk)),
+            pltpu.SemaphoreType.DMA((2, 7)),
+        ],
+        compiler_params=pltpu.CompilerParams(
+            collective_id=number, has_side_effects=True, vmem_limit_bytes=24 * 2**20
+        ),
+    )(order, loc, pool)
+
+
+def finish_kernel(
+    caps,
+    chunk,
+    mate_ref,
+    con_ref,
+    fin_ref,
+    ge_ref,
+    dw_ref,
+    gs_ref,
+    gw_ref,
+    taken,
+    comb,
+    outb,
+    inb,
+    done,
+    pair_in,
+    held,
+    y_half,
+    y_in,
+    x_half,
+    x_in,
+    z_in,
+    team_sem,
+    ring_sem,
+    home_sem,
+    core_sem,
+    y_sem,
+    x_sem,
+    z_sem,
+):
+    z, x, y, core = place()
+    me = x * 2 + core
+    total = sum(caps)
+    first = starts(caps)
+    friends = [teammate(z, y, (me + k) % 8) for k in range(1, 8)]
+    around = [at(z + k, x, y, core) for k in range(1, 8)]
+    ahead = around[0]
+    behind = around[6]
+    sides = [at(z, x, y + 1, core), at(z, x, y - 1, core)]
+    greet(friends + around + sides)
+
     def send(src, dst, sems, slot, target):
-        copy = pltpu.make_async_remote_copy(
-            src_ref=src,
-            dst_ref=dst,
-            send_sem=sems.at[0, slot],
-            recv_sem=sems.at[1, slot],
-            device_id=target,
-            device_id_type=MESH,
-        )
-        copy.start()
-        return copy
-
+        return push(src, dst, sems.at[0, slot], sems.at[1, slot], target)
+
+    given = []
+    for k in range(1, 8):
+        member = (me + k) % 8
+        given.append(
+            send(
+                ge_ref.at[:, pl.ds(pl.multiple_of(member * 16, 16), 16), :],
+                taken.at[pl.ds(me * 4, 4)],
+                team_sem,
+                k - 1,
+                friends[k - 1],
+            )
+        )
     offsets = (2, 1, 3, 0)
+    partner = at(z, x, y, 1 - core)
     swaps = []
     for slot, offset in enumerate(offsets):
         theirs = (y + offset) % 4 * 2 + 1 - core
-        swaps.append(
-            send(dw_ref.at[theirs], pair_in.at[slot], core_sem, slot, at(z, x, y, 1 - core))
-        )
+        swaps.append(send(dw_ref.at[theirs], pair_in.at[slot], core_sem, slot, partner))
+    taken[pl.ds(me * 4, 4)] = ge_ref[:, pl.ds(pl.multiple_of(me * 16, 16), 16), :]
+    taken[32] = jnp.zeros((16, 512), BF)
+    comb[32] = jnp.zeros((16, 512), F32)
+    inb[2 * total] = jnp.zeros((16, 512), BF)
+    for copy in given:
+        copy.wait_recv()
+
+    def combine(i, carry):
+        row = taken[mate_ref[i, 0]].astype(F32)
+        for t in range(1, 4):
+            row = row + taken[mate_ref[i, t]].astype(F32)
+        comb[i] = row
+        return carry
+
+    lax.fori_loop(0, 32, combine, 0)
+    copies = {}
+
+    def back(r, i, added):
+        for d in range(2):
+            slot = d * total + first[r] + i * chunk
+            if added:
+                copies[d, r + 1, i].wait_recv()
+                further = d * total + first[r + 1] + i * chunk
+
+                def fill(j, carry, d=d, slot=slot, further=further):
+                    outb[slot + j] = (
+                        comb[con_ref[d, r, i * chunk + j]] + inb[further + j].astype(F32)
+                    ).astype(BF)
+                    return carry
+            else:
+
+                def fill(j, carry, d=d, slot=slot):
+                    outb[slot + j] = comb[con_ref[d, r, i * chunk + j]].astype(BF)
+                    return carry
+
+            lax.fori_loop(0, chunk, fill, 0)
+            index = (first[r] + i * chunk) // chunk
+            copies[d, r, i] = push(
+                outb.at[pl.ds(slot, chunk)],
+                inb.at[pl.ds(slot, chunk)],
+                ring_sem.at[0, d, index],
+                ring_sem.at[1, d, index],
+                behind if d == 0 else ahead,
+            )
+
+    for i in range(caps[3] // chunk):
+        back(3, i, False)
+    for r in (2, 1, 0):
+        for i in range(caps[r + 1] // chunk, caps[r] // chunk):
+            back(r, i, False)
 
     def add_pair(slot, offset):
         swaps[slot].wait_recv()
@@ -169,21 +471,55 @@
             ).astype(BF)
 
     add_pair(0, 2)
-    up = send(held.at[0, pl.ds(0, 2)], y_half.at[0], y_sem, 0, at(z, x, y + 1, core))
-    down = send(held.at[0, pl.ds(2, 2)], y_half.at[1], y_sem, 1, at(z, x, y - 1, core))
+    up = send(held.at[0, pl.ds(0, 2)], y_half.at[0], y_sem, 0, sides[0])
+    down = send(held.at[0, pl.ds(2, 2)], y_half.at[1], y_sem, 1, sides[1])
+    for i in range(caps[3] // chunk):
+        back(2, i, True)
     add_pair(1, 1)
     add_pair(2, 3)
     add_pair(3, 0)
+    for i in range(caps[2] // chunk):
+        back(1, i, True)
     up.wait_recv()
     for part in range(2):
         held[1, part] = (held[1, part].astype(F32) + y_half[0, part].astype(F32)).astype(BF)
-    up2 = send(held.at[1], y_in.at[0], y_sem, 2, at(z, x, y + 1, core))
+    up2 = send(held.at[1], y_in.at[0], y_sem, 2, sides[0])
     down.wait_recv()
     for part in range(2):
         held[2, part + 2] = (
             held[2, part + 2].astype(F32) + y_half[1, part].astype(F32)
         ).astype(BF)
-    down2 = send(held.at[2], y_in.at[1], y_sem, 3, at(z, x, y - 1, core))
+    down2 = send(held.at[2], y_in.at[1], y_sem, 3, sides[1])
+    for i in range(caps[1] // chunk):
+        back(0, i, True)
+    for i in range(caps[0] // chunk):
+        for d in range(2):
+            copies[d, 0, i].wait_recv()
+
+    def close(i, carry):
+        for k in range(8):
+            b = i * 8 + k
+            done[i, k] = (
+                inb[fin_ref[b, 0]].astype(F32)
+                + inb[fin_ref[b, 1]].astype(F32)
+                + comb[fin_ref[b, 2]]
+            ).astype(BF)
+        return carry
+
+    lax.fori_loop(0, 8, close, 0)
+    rows = pl.ds(pl.multiple_of(me * 16, 16), 16)
+    homes = []
+    for k in range(1, 8):
+        homes.append(
+            send(
+                done.at[(me + k) % 8],
+                gs_ref.at[:, rows, :],
+                home_sem,
+                k - 1,
+                friends[k - 1],
+            )
+        )
+    gs_ref[:, rows, :] = done[me]
     up2.wait_recv()
     down2.wait_recv()
 
@@ -195,20 +531,22 @@
             + y_in[1, part].astype(F32)
         )
 
+    left = at(z, x - 1, y, core)
+    right = at(z, x + 1, y, core)
     held[4, 0] = y_total(2).astype(BF)
-    xup = send(held.at[4, 0, 0], x_half.at[0], x_sem, 0, at(z, x + 1, y, core))
-    xdown = send(held.at[4, 0, 1], x_half.at[1], x_sem, 1, at(z, x - 1, y, core))
-    ahead = y_total(1)
-    behind = y_total(3)
+    xup = send(held.at[4, 0, 0], x_half.at[0], x_sem, 0, right)
+    xdown = send(held.at[4, 0, 1], x_half.at[1], x_sem, 1, left)
+    ahead_x = y_total(1)
+    behind_x = y_total(3)
     own = y_total(0)
     xup.wait_recv()
-    held[4, 1, 0] = (ahead[0] + x_half[0].astype(F32)).astype(BF)
-    held[4, 1, 1] = ahead[1].astype(BF)
-    xup2 = send(held.at[4, 1], x_in.at[0], x_sem, 2, at(z, x + 1, y, core))
+    held[4, 1, 0] = (ahead_x[0] + x_half[0].astype(F32)).astype(BF)
+    held[4, 1, 1] = ahead_x[1].astype(BF)
+    xup2 = send(held.at[4, 1], x_in.at[0], x_sem, 2, right)
     xdown.wait_recv()
-    held[4, 2, 0] = behind[0].astype(BF)
-    held[4, 2, 1] = (behind[1] + x_half[1].astype(F32)).astype(BF)
-    xdown2 = send(held.at[4, 2], x_in.at[1], x_sem, 3, at(z, x - 1, y, core))
+    held[4, 2, 0] = behind_x[0].astype(BF)
+    held[4, 2, 1] = (behind_x[1] + x_half[1].astype(F32)).astype(BF)
+    xdown2 = send(held.at[4, 2], x_in.at[1], x_sem, 3, left)
     xup2.wait_recv()
     xdown2.wait_recv()
     held[4, 3] = (own + x_in[0].astype(F32) + x_in[1].astype(F32)).astype(BF)
@@ -217,26 +555,38 @@
     for step in (4, 3, 5, 2, 6, 1, 7):
         target = (z + step) % 8
         zs.append(
-            send(
-                held.at[4, 3, :, target], z_in.at[step - 1], z_sem, step - 1, at(z + step, x, y, core)
-            )
+            send(held.at[4, 3, :, target], z_in.at[step - 1], z_sem, step - 1, around[step - 1])
         )
     result = held[4, 3, :, z].astype(F32)
     for copy, step in zip(zs, (4, 3, 5, 2, 6, 1, 7)):
         copy.wait_recv()
         result = result + z_in[step - 1].astype(F32)
-    out_ref[...] = result
-    for copy in swaps + [up, down, up2, down2, xup, xdown, xup2, xdown2] + zs:
+    gw_ref[...] = result
+    for copy in homes:
+        copy.wait_recv()
+    rest = swaps + [up, down, up2, down2, xup, xdown, xup2, xdown2] + zs
+    for copy in given + homes + rest + list(copies.values()):
         copy.wait_send()
 
 
-def reduce_weights(dw):
+def finish(caps, chunk, number, mate, con, fin, ge, dw):
+    total = sum(caps)
+    smem = pl.BlockSpec(memory_space=pltpu.SMEM)
+    vmem = pl.BlockSpec(memory_space=pltpu.VMEM)
     return pl.pallas_call(
-        reduce_kernel,
-        in_specs=[pl.BlockSpec(memory_space=pltpu.VMEM)],
-        out_specs=pl.BlockSpec(memory_space=pltpu.VMEM),
-        out_shape=jax.ShapeDtypeStruct((2, 16, 256), F32),
+        functools.partial(finish_kernel, caps, chunk),
+        in_specs=[smem, smem, smem, vmem, vmem],
+        out_specs=[vmem, vmem],
+        out_shape=[
+            jax.ShapeDtypeStruct((8, 128, 512), BF),
+            jax.ShapeDtypeStruct((2, 16, 256), F32),
+        ],
         scratch_shapes=[
+            pltpu.VMEM((33, 16, 512), BF),
+            pltpu.VMEM((33, 16, 512), F32),
+            pltpu.VMEM((2 * total, 16, 512), BF),
+            pltpu.VMEM((2 * total + 1, 16, 512), BF),
+            pltpu.VMEM((8, 8, 16, 512), BF),
             pltpu.VMEM((4, 4, 2, 8, 16, 256), BF),
             pltpu.VMEM((5, 4, 2, 8, 16, 256), BF),
             pltpu.VMEM((2, 2, 2, 8, 16, 256), BF),
@@ -244,49 +594,131 @@
             pltpu.VMEM((2, 8, 16, 256), BF),
             pltpu.VMEM((2, 2, 8, 16, 256), BF),
             pltpu.VMEM((7, 2, 16, 256), BF),
+            pltpu.SemaphoreType.DMA((2, 7)),
+            pltpu.SemaphoreType.DMA((2, 2, total // chunk)),
+            pltpu.SemaphoreType.DMA((2, 7)),
             pltpu.SemaphoreType.DMA((2, 4)),
             pltpu.SemaphoreType.DMA((2, 4)),
             pltpu.SemaphoreType.DMA((2, 4)),
             pltpu.SemaphoreType.DMA((2, 7)),
         ],
         compiler_params=pltpu.CompilerParams(
-            collective_id=1, has_side_effects=True, vmem_limit_bytes=40 * 2**20
+            collective_id=number, has_side_effects=True, vmem_limit_bytes=48 * 2**20
         ),
-    )(dw)
+    )(mate, con, fin, ge, dw)
+
+
+TIGHT = (24, 20, 16, 8)
+WIDE = (64, 64, 64, 32)
+
+
+def plan(ids):
+    z, x, y, core = place()
+    i32 = jnp.int32
+    member_core = jnp.arange(8, dtype=i32)[None, None, :, None] % 2
+    block = (ids // 8 % 4 * 2 + member_core) * 8 + ids % 8
+    owner_z = ids // 32
+    away = (jnp.arange(8, dtype=i32)[None, :, None, None] - owner_z + 8) % 8
+    flat = (owner_z * 64 + block).reshape(4, 256)
+    is_block = (flat[:, None, :] == jnp.arange(512, dtype=i32)[None, :, None]).astype(BF)
+    is_away = (away.reshape(4, 1, 256) == jnp.arange(8, dtype=i32)[None, :, None]).astype(BF)
+    wanted = jnp.einsum("ydr,ybr->ydb", is_away, is_block, preferred_element_type=F32) > 0.5
+    wanted = wanted.reshape(4, 8, 8, 64)
+    team = jnp.arange(64, dtype=i32)
+    even = team % 2 == 0
+
+    def far(one, two, three, four):
+        return jnp.where(four, 4, jnp.where(three, 3, jnp.where(two, 2, jnp.where(one, 1, 0))))
+
+    up = far(wanted[:, 1], wanted[:, 2], wanted[:, 3], wanted[:, 4] & even)
+    down = far(wanted[:, 7], wanted[:, 6], wanted[:, 5], wanted[:, 4] & ~even)
+    fars = jnp.stack([up, down], axis=1).astype(i32)
+    lengths = jnp.stack(
+        [jnp.max(jnp.sum((fars >= r).astype(i32), axis=-1)) for r in range(1, 5)]
+    )
+    fits = jnp.all(lengths <= jnp.array(TIGHT, i32))
+    fars = lax.dynamic_index_in_dim(fars, y, 0, keepdims=False)
+    fars = lax.dynamic_slice_in_dim(jnp.concatenate([fars, fars], axis=1), z, 8, axis=1)
+    key = fars * 64 + 63 - team
+    rank = jnp.sum((key[..., None, :] > key[..., :, None]).astype(i32), axis=-1)
+    at_rank = rank[..., None, :] == team[:, None]
+    order = jnp.sum(jnp.where(at_rank[:, 0], team, 0), axis=-1)
+
+    def mine(a):
+        a = lax.dynamic_index_in_dim(a, y, 0, keepdims=False)
+        return lax.dynamic_index_in_dim(a, z, 0, keepdims=False).reshape(32)
+
+    my_block, my_away = mine(block), mine(away)
+    my_flat = (8 - my_away) % 8 * 64 + my_block
+    upwards = (my_away < 4) | ((my_away == 4) & (my_block % 2 == 0))
+    hops = jnp.where(upwards, my_away, 8 - my_away)
+    hit = my_flat[:, None] == jnp.arange(512, dtype=i32)[None, :]
+    ranks = jnp.sum(jnp.where(hit[None], rank.reshape(2, 1, 512), 0), axis=-1)
+    spot = jnp.where(upwards, ranks[0], ranks[1])
+    refs = jnp.arange(32, dtype=i32)
+    first = jnp.min(jnp.where(hit, refs[:, None], 32), axis=0).reshape(8, 64)
+    same = my_flat[:, None] == my_flat[None, :]
+    earlier = jnp.sum((same[:, None, :] & (refs[None, None, :] < refs[None, :, None])).astype(i32), axis=-1)
+    mate = 32 + jnp.sum(
+        jnp.where(
+            same[:, None, :] & (earlier[:, None, :] == jnp.arange(4, dtype=i32)[None, :, None]),
+            refs - 32,
+            0,
+        ),
+        axis=-1,
+    )
+    firsts = jnp.stack(
+        [
+            jnp.stack([first[7], first[6], first[5], jnp.where(even, first[4], 32)]),
+            jnp.stack([first[1], first[2], first[3], jnp.where(even, 32, first[4])]),
+        ]
+    )
+    at_rank_by_hop = jnp.stack(
+        [
+            jnp.stack([at_rank[0, 7], at_rank[0, 6], at_rank[0, 5], at_rank[0, 4]]),
+            jnp.stack([at_rank[1, 1], at_rank[1, 2], at_rank[1, 3], at_rank[1, 4]]),
+        ]
+    )
+    con = 32 + jnp.sum(jnp.where(at_rank_by_hop, firsts[:, :, None, :] - 32, 0), axis=-1)
+
+    def locate(caps):
+        total = sum(caps)
+        offset = sum(jnp.where(hops == r + 1, starts(caps)[r], 0) for r in range(4))
+        there = jnp.where(upwards, 0, total) + offset + spot
+        return jnp.where(my_away == 0, 2 * total + my_block, there)
+
+    def collect(caps):
+        total = sum(caps)
+        return jnp.stack(
+            [
+                jnp.where(fars[0, 0] > 0, rank[0, 0], 2 * total),
+                jnp.where(fars[1, 0] > 0, total + rank[1, 0], 2 * total),
+                first[0],
+            ],
+            axis=1,
+        )
+
+    return fits, order, mate, con, locate, collect
 
 
 def body(queries, grad_out, enc_states, neighbour_ids, kv_weight):
-    seq_count = lax.axis_size("seq")
-    blocks_dev = enc_states.shape[1]
-    nbr_len = enc_states.shape[2]
-    enc_width = enc_states.shape[3]
-    flat_refs = neighbour_ids.reshape(-1)
-    ref_count = flat_refs.shape[0]
-    owners = flat_refs // blocks_dev
-    local_slot = flat_refs % blocks_dev
-    placing = owners[:, None] == jnp.arange(seq_count)[None, :]
-    wanted = jnp.sum(jnp.where(placing, local_slot[:, None] + 1, 0), axis=0) - 1
-    asked = lax.all_to_all(
-        wanted.reshape(seq_count, 1), "seq", split_axis=0, concat_axis=0, tiled=True
-    ).reshape(-1)
-    replies = jnp.take(enc_states[0], jnp.maximum(asked, 0), axis=0)
-    arrived = lax.all_to_all(replies, "seq", split_axis=0, concat_axis=0, tiled=True)
-    states = jnp.take(arrived, owners, axis=0)
-    flat_states = states.reshape(ref_count * nbr_len, enc_width)
-    gq, grad_e, dw = attention(flat_states, kv_weight, queries[0], grad_out[0])
-    grad_weight = reduce_weights(dw)
-    placing_b = placing.astype(BF)
-    grad_e = grad_e.reshape(ref_count, nbr_len, enc_width)
-    sending = jnp.einsum("rs,rtc->stc", placing_b, grad_e, preferred_element_type=F32).astype(BF)
-    picking = (asked[:, None] == jnp.arange(blocks_dev)[None, :]).astype(BF)
-    summed = jnp.einsum(
-        "sb,stc->btc",
-        picking,
-        lax.all_to_all(sending, "seq", split_axis=0, concat_axis=0, tiled=True),
-        preferred_element_type=F32,
-    )
-    grad_states = summed.astype(BF)[None]
-    return (gq[None], grad_states, grad_weight)
+    row = jnp.pad(neighbour_ids.reshape(1, 4), ((0, 0), (0, 124)))
+    pool, ids = spread(row, enc_states[0])
+    fits, order, mate, con, locate, collect = plan(ids[:, :, :, 0, :4])
+    pool = pool.reshape(64, 16, 512)
+    states = lax.cond(
+        fits,
+        lambda: gather(TIGHT, 4, 2, order, locate(TIGHT), pool),
+        lambda: gather(WIDE, 16, 3, order, locate(WIDE), pool),
+    )
+    gq, grad_e, dw = attention(states.reshape(512, 512), kv_weight, queries[0], grad_out[0])
+    grad_e = grad_e.reshape(4, 128, 512)
+    grad_states, grad_weight = lax.cond(
+        fits,
+        lambda: finish(TIGHT, 4, 4, mate, con, collect(TIGHT), grad_e, dw),
+        lambda: finish(WIDE, 16, 5, mate, con, collect(WIDE), grad_e, dw),
+    )
+    return (gq[None], grad_states[None], grad_weight)
 
 
 def solution(mesh):

time: 269 us -> 167 us (0.62); the launches traced: 264 us -> 166 us
  waiting for transfers between devices: 92.5 us -> 0 us
  Pallas kernels: 107 us -> 147 us
  blocking collectives: 20.2 us -> 0 us
  local copies, waits for them, and re-layouts: 19.3 us -> 7.04 us
  starting transfers between devices: 12 us -> 0 us
  matrix products: 5.93 us -> 0.46 us
  other arithmetic: 6.15 us -> 10.6 us
    all_to_all x2 -> x0, waiting for transfers between devices: 92.5 us -> none  [the longest x1 92.5 us: body(): lax.all_to_all(replies, 'seq', split_axis=0, concat_axis=0, tiled=True)]
    pallas_call x1 -> x3, Pallas kernels: 89.6 us -> 129 us  [the longest x1 64.6 us: finish(): pl.pallas_call(functools.partial(finish_kernel, caps, chunk), in_specs=[s...]
    all_to_all x1 -> x0, blocking collectives: 20.2 us -> none  [body(): lax.all_to_all(wanted.reshape(seq_count, 1), 'seq', split_axis=0, concat_...]
    all_to_all x2 -> x0, starting transfers between devices: 12 us -> none  [the longest x1 6.98 us: body(): lax.all_to_all(sending, 'seq', split_axis=0, concat_axis=0, tiled=True)]
    gather x2 -> x0, local copies, waits for them, and re-layouts: 5.56 us -> none  [the longest x1 2.79 us: body(): replies = jnp.take(enc_states[0], jnp.maximum(asked, 0), axis=0)]
    dot_general x2 -> x1, matrix products: 5.93 us -> 0.46 us  [plan(): jnp.einsum('ydr,ybr->ydb', is_away, is_block, preferred_element_type=F32)]
    select_n x3 -> x6, other arithmetic: 4.78 us -> 0.14 us  [the longest x2 0.11 us: plan(): away = (jnp.arange(8, dtype=i32)[None, :, None, None] - owner_z + 8) % 8]
    convert_element_type x1 -> x0, local copies, waits for them, and re-layouts: 4.37 us -> none  [body(): jnp.einsum('rs,rtc->stc', placing_b, grad_e, preferred_element_type=F32)]
  transfers between devices with their start and end apart: 2 -> 0, of which waited for: 1 -> 0; matrix products, arithmetic and copies ran while one was open for 0% -> 0% of each run, Pallas kernels for 34% -> 0%
where the time goes in v2:
time: 167 us; the launch traced here: 166 us
  Pallas kernels  147 us (88%)
  other arithmetic  10.6 us (6%)
  local copies, waits for them, and re-layouts  7.04 us (4%)
    pallas_call x1, Pallas kernels, finish(): pl.pallas_call(functools.partial(finish_kernel, caps, chunk), in_specs=[s...  64.6 us
    pallas_call x1, Pallas kernels, gather(): pl.pallas_call(functools.partial(gather_kernel, caps, chunk), in_specs=[p...  41.1 us
    pallas_call x1, Pallas kernels, spread(): pl.pallas_call(spread_kernel, in_specs=[pl.BlockSpec(memory_space=pltpu.V...  23.2 us
    pallas_call x1, Pallas kernels, attention(): pl.pallas_call(attention_kernel, grid=(8,), in_specs=[pl.BlockSpec((keys,...  17.7 us
    unnamed x10, local copies, waits for them, and re-layouts  5 us
    reduce_and x1, other arithmetic, plan(): fits = jnp.all(lengths <= jnp.array(TIGHT, i32))  3.99 us

profile of v2, /device:TPU:1, one launch (start us, length us, event | category | flops | bytes accessed | tf_op | source)
XLA Modules:
  0.0 166.3 jit_solution(18213385492874960975)
XLA Ops:
  0.7 0.8 reshape.434
  1.5 0.1 add.302
  1.5 0.1 add.303
  1.7 0.1 sub.82
  1.8 0.0 copy-start
  1.8 1.2 copy-done
  3.0 0.0 copy-start.2
  3.0 0.0 copy-start.3
  3.0 23.2 %shard_map.85 = (bf16[8,8,16,512]{3,2,1,0:T(8,128)(2,1)S(1)}, s32[4,8,8,1,128]{4,3,2,1,0:T(1,128)S(1)}) custom-call(s32[1,128]{1,0:T(1,128)S(1)} %pad.4.row_ref, bf16[8,128,512]{2,1,0:T(8,128)(2,1)S(1)} %bitcast.107), custom_call_target="tpu_custom_call" | custom-call | tf_op jit(solution)/shard_map/pallas_call | solution.py:221
  26.3 0.4 fusion.43
  26.7 0.1 squeeze.78
  26.8 0.5 fusion.13
  27.3 0.1 reshape.435
  27.5 0.6 convert_reduce_fusion.4
  28.1 0.6 reduce_max.39
  28.8 0.6 reduce_max.38
  29.4 0.6 reduce_max.37
  30.0 0.7 reduce_max.36
  30.8 4.0 %compare_reduce_fusion = pred[]{:T(512)} fusion(s32[4]{0:T(128)} %constant.308.clone, s32[1]{0:T(128)} %bitcast.28, s32[1]{0:T(128)} %bitcast.27, s32[1]{0:T(128)} %bitcast.26, s32[1]{0:T(128)} %bitcast.25), kind=kLoop, calls=%fused_computation.152 | loop fusion | flops 19 | bytes 33 | tf_op jit(solution)/shard_map/reduce_and | solution.py:639
  35.3 0.5 convert_reduce_fusion
  35.9 0.1 broadcast_in_dim.227
  35.9 0.1 iota_compare_fusion.4
  36.1 0.2 broadcast_compare_fusion.2
  36.4 0.1 negate_select_fusion.3
  36.5 0.1 add_select_fusion.4
  36.6 0.1 reshape.436
  36.7 0.1 reshape.437
  36.8 0.1 select_reduce_fusion.7
  36.9 0.1 broadcast_compare_fusion.4
  37.0 0.1 slice_bitcast_fusion.17
  37.1 0.1 iota_compare_fusion.5
  37.2 0.1 select_reduce_fusion.6
  37.3 41.2 %conditional.2 = (bf16[512,512]{1,0:T(8,128)(2,1)S(1)}) conditional(s32[]{:T(128)} %convert_element_type.28, (pred[2,8,64,64]{3,2,1,0:T(8,128)(4,1)S(1)}, s32[2,64,64]{2,1,0:T(8,128)S(1)}, s32[32]{0:T(128)S(1)}, s32[32]{0:T(128)S(1)}, pred[32]{0:T(512)(128)(4,1)S(1)}, /*index=5*/s32[2,32]{1,0:T(2,128)S(1)}, ...), branch_computations={%region_11.13_spmd, %region_13.15_spmd} | conditional | flops 16800 | bytes 83112 | solution.py:709
  37.3 0.1 select_reduce_fusion.1.order_ref
  37.4 41.1 %branch_1_fun.4 = bf16[4,128,512]{2,1,0:T(8,128)(2,1)S(1)} custom-call(s32[2,64]{1,0:T(2,128)S(1)} %select_reduce_fusion.1.order_ref, s32[32]{0:T(128)S(1)} %compare_select_fusion.7.loc_ref, bf16[64,16,512]{2,1,0:T(8,128)(2,1)S(1)} %bitcast.111), custom_call_target="tpu_custom_call" | custom-call | tf_op jit(solution)/shard_map/cond/branch_1_fun/pallas_call | solution.py:330
  78.5 0.1 and_convert_fusion
  78.6 0.0 copy-done.2
  78.6 0.0 copy-done.3
  78.6 0.0 copy-start.1
  78.6 2.2 %copy-done.1 = bf16[2,512,2048]{2,1,0:T(8,128)(2,1)S(1)} copy-done((bf16[2,512,2048]{2,1,0:T(8,128)(2,1)S(1)}, bf16[2,512,2048]{2,1,0:T(8,128)(2,1)}, u32[]{:S(2)}) %copy-start.1) | copy-done | bytes 4194328
  80.8 17.7 %shard_map.86 = (bf16[128,2048]{1,0:T(8,128)(2,1)}, bf16[512,512]{1,0:T(8,128)(2,1)S(1)}, bf16[8,4,2,8,16,256]{5,4,3,2,1,0:T(8,128)(2,1)}) custom-call(bf16[512,512]{1,0:T(8,128)(2,1)S(1)} %get-tuple-element.544.states_ref, bf16[2,512,2048]{2,1,0:T(8,128)(2,1)S(1)} %copy-done.1, bf16[128,2048]{1,0:T(8,128)(2,1)S(1)} %bitcast.108, bf16[128,2048]{1,0:T(8,128)(2,1)S(1)} %bitcast.109), custom_call_target="tpu_custom_call" | custom-call | flops 7200000000 | bytes 12000000 | tf_op jit(solution)/shard_map/pallas_call | solution.py:91
  98.5 66.2 %conditional.3 = (f32[2,16,256]{2,1,0:T(8,128)S(1)}, bf16[1,8,128,512]{3,2,1,0:T(8,128)(2,1)S(1)}) conditional(s32[]{:T(128)} %convert_element_type.28, (pred[32,32]{1,0:T(8,128)(4,1)S(1)}, s32[32,32,32]{2,1,0:T(8,128)S(1)}, s32[32,4,32]{2,1,0:T(4,128)S(1)}, s32[32]{0:T(128)S(1)}, s32[2,4,1,64]{3,1,2,0:T(4,128)S(1)}, ...), branch_computations={%region_16.20_spmd, %region_20.24_spmd} | conditional | flops 114912 | bytes 208788 | solution.py:716
  98.5 0.2 select_reduce_fusion.4
  98.8 0.6 reduce_sum.117
  99.4 0.6 select_reduce_fusion.5
  100.0 0.1 copy.44.fin_ref
  100.1 64.6 %branch_1_fun.5 = (bf16[8,128,512]{2,1,0:T(8,128)(2,1)S(1)}, f32[2,16,256]{2,1,0:T(8,128)S(1)}) custom-call(s32[32,4]{1,0:T(8,128)S(1)} %broadcast_add_fusion.4.mate_ref, s32[2,4,64]{2,1,0:T(4,128)S(1)} %broadcast_add_fusion.6.con_ref, s32[64,3]{1,0:T(8,128)S(1)} %copy.44.fin_ref, bf16[4,128,512]{2,1,0:T(8,128)(2,1)S(1)} %bitcast.113, ...), custom_call_target="tpu_custom_call" | custom-call | tf_op jit(solution)/shard_map/cond/branch_1_fun/pallas_call | solution.py:576
  164.7 1.0 copy.67
  165.7 0.6 copy.68
  (30 shorter events, 0.3 us)
Async XLA Ops:
  1.8 1.2 copy-start
  3.0 75.6 %copy-start.2 = (bf16[1,128,2048]{2,1,0:T(8,128)(2,1)S(1)}, bf16[1,128,2048]{2,1,0:T(8,128)(2,1)}, u32[]{:S(2)}) copy-start(bf16[1,128,2048]{2,1,0:T(8,128)(2,1)} %param.10) | copy-start | bytes 1572868
  3.0 75.6 %copy-start.3 = (bf16[1,128,2048]{2,1,0:T(8,128)(2,1)S(1)}, bf16[1,128,2048]{2,1,0:T(8,128)(2,1)}, u32[]{:S(2)}) copy-start(bf16[1,128,2048]{2,1,0:T(8,128)(2,1)} %param.11) | copy-start | bytes 1572868
  78.6 2.2 %copy-start.1 = (bf16[2,512,2048]{2,1,0:T(8,128)(2,1)S(1)}, bf16[2,512,2048]{2,1,0:T(8,128)(2,1)}, u32[]{:S(2)}) copy-start(bf16[2,512,2048]{2,1,0:T(8,128)(2,1)} %w_ref.1) | copy-start | bytes 12582916

commit v3 on v2

--- a/solution.py
+++ b/solution.py
@@ -108,7 +108,7 @@
             jax.ShapeDtypeStruct((8, 4, 2, 8, 16, 256), BF),
         ],
         scratch_shapes=[pltpu.VMEM((enc, keys), BF), pltpu.VMEM((keys, enc), F32)],
-        compiler_params=pltpu.CompilerParams(vmem_limit_bytes=40 * 2**20),
+        compiler_params=pltpu.CompilerParams(vmem_limit_bytes=60 * 2**20),
         cost_estimate=pl.CostEstimate(
             flops=7_200_000_000, bytes_accessed=12_000_000, transcendentals=600_000
         ),
@@ -173,7 +173,7 @@
         member = (me + k) % 8
         pieces.append(
             push(
-                enc_ref.at[:, pl.ds(pl.multiple_of(member * 16, 16), 16), :],
+                enc_ref.at[:, pl.ds(pl.multiple_of(member * 16, 16), 16), pl.ds(0, 256)],
                 pool_ref.at[me],
                 team_sem.at[0, k - 1],
                 team_sem.at[1, k - 1],
@@ -181,7 +181,9 @@
             )
         )
     own = pltpu.make_async_copy(
-        enc_ref.at[:, pl.ds(pl.multiple_of(me * 16, 16), 16), :], pool_ref.at[me], own_sem
+        enc_ref.at[:, pl.ds(pl.multiple_of(me * 16, 16), 16), pl.ds(0, 256)],
+        pool_ref.at[me],
+        own_sem,
     )
     own.start()
     for copy in rows:
@@ -229,7 +231,7 @@
             pl.BlockSpec(memory_space=pltpu.VMEM),
         ],
         out_shape=[
-            jax.ShapeDtypeStruct((8, 8, 16, 512), BF),
+            jax.ShapeDtypeStruct((8, 8, 16, 256), BF),
             jax.ShapeDtypeStruct((4, 8, 8, 1, 128), jnp.int32),
         ],
         scratch_shapes=[
@@ -250,7 +252,23 @@
 
 
 def gather_kernel(
-    caps, chunk, order_ref, loc_ref, pool_ref, states_ref, packed, arr, stage, ring_sem, team_sem
+    caps,
+    chunk,
+    order_ref,
+    loc_ref,
+    pool_ref,
+    enc_ref,
+    states_ref,
+    pool1,
+    packed,
+    arr0,
+    arr1,
+    stage0,
+    stage1,
+    ring_sem,
+    team_sem,
+    spread_sem,
+    own_sem,
 ):
     z, x, y, core = place()
     me = x * 2 + core
@@ -259,73 +277,112 @@
     friends = [teammate(z, y, (me + k) % 8) for k in range(1, 8)]
     ahead = at(z + 1, x, y, core)
     behind = at(z - 1, x, y, core)
+    own = pltpu.make_async_copy(
+        enc_ref.at[:, pl.ds(pl.multiple_of(me * 16, 16), 16), pl.ds(256, 256)],
+        pool1.at[pl.ds(pl.multiple_of(me * 8, 8), 8)],
+        own_sem,
+    )
+    own.start()
     greet(friends + [ahead, behind])
     copies = {}
-
-    def forward(d, r, i, src):
+    arrs = (arr0, arr1)
+    stages = (stage0, stage1)
+
+    def forward(h, d, r, i, src):
         slot = first[r] + i * chunk
         index = slot // chunk
-        copies[d, r, i] = push(
+        copies[h, d, r, i] = push(
             src,
-            arr.at[pl.ds(d * total + slot, chunk)],
-            ring_sem.at[0, d, index],
-            ring_sem.at[1, d, index],
+            arrs[h].at[pl.ds(d * total + slot, chunk)],
+            ring_sem.at[0, h, d, index],
+            ring_sem.at[1, h, d, index],
             ahead if d == 0 else behind,
         )
 
-    for i in range(caps[0] // chunk):
-        for d in range(2):
-
-            def fill(j, carry, i=i, d=d):
-                packed[d, i * chunk + j] = pool_ref[order_ref[d, i * chunk + j]]
-                return carry
-
-            lax.fori_loop(0, chunk, fill, 0)
-            forward(d, 0, i, packed.at[d, pl.ds(i * chunk, chunk)])
-
-    def keep(j, carry):
-        arr[2 * total + j] = pool_ref[j]
-        return carry
-
-    lax.fori_loop(0, 64, keep, 0)
-    for r in range(1, 4):
+    def first_hop(h, pool):
+        for i in range(caps[0] // chunk):
+            for d in range(2):
+
+                def fill(j, carry, i=i, d=d):
+                    packed[h, d, i * chunk + j] = pool[order_ref[d, i * chunk + j]]
+                    return carry
+
+                lax.fori_loop(0, chunk, fill, 0, unroll=4)
+                forward(h, d, 0, i, packed.at[h, d, pl.ds(i * chunk, chunk)])
+
+        def keep(j, carry):
+            arrs[h][2 * total + j] = pool[j]
+            return carry
+
+        lax.fori_loop(0, 64, keep, 0, unroll=8)
+
+    def next_hop(h, r):
         for i in range(caps[r] // chunk):
             for d in range(2):
-                copies[d, r - 1, i].wait_recv()
+                copies[h, d, r - 1, i].wait_recv()
                 slot = d * total + first[r - 1] + i * chunk
-                forward(d, r, i, arr.at[pl.ds(slot, chunk)])
-    for r in range(4):
-        low = caps[r + 1] // chunk if r < 3 else 0
-        for i in range(low, caps[r] // chunk):
-            for d in range(2):
-                copies[d, r, i].wait_recv()
-
-    def pick(i, carry):
-        for k in range(4):
-            stage[i, k] = arr[loc_ref[i * 4 + k]]
-        return carry
-
-    lax.fori_loop(0, 8, pick, 0)
+                forward(h, d, r, i, arrs[h].at[pl.ds(slot, chunk)])
+
     rows = pl.ds(pl.multiple_of(me * 16, 16), 16)
     hands = []
+
+    def hand_out(h):
+        for r in range(4):
+            low = caps[r + 1] // chunk if r < 3 else 0
+            for i in range(low, caps[r] // chunk):
+                for d in range(2):
+                    copies[h, d, r, i].wait_recv()
+
+        def pick(i, carry):
+            for k in range(4):
+                stages[h][i, k] = arrs[h][loc_ref[i * 4 + k]]
+            return carry
+
+        lax.fori_loop(0, 8, pick, 0)
+        for k in range(1, 8):
+            hands.append(
+                push(
+                    stages[h].at[(me + k) % 8],
+                    states_ref.at[:, rows, pl.ds(h * 256, 256)],
+                    team_sem.at[0, h, k - 1],
+                    team_sem.at[1, h, k - 1],
+                    friends[k - 1],
+                )
+            )
+        states_ref[:, rows, h * 256 : h * 256 + 256] = stages[h][me]
+
+    first_hop(0, pool_ref)
+    pieces = []
     for k in range(1, 8):
-        hands.append(
+        member = (me + k) % 8
+        pieces.append(
             push(
-                stage.at[(me + k) % 8],
-                states_ref.at[:, rows, :],
-                team_sem.at[0, k - 1],
-                team_sem.at[1, k - 1],
+                enc_ref.at[:, pl.ds(pl.multiple_of(member * 16, 16), 16), pl.ds(256, 256)],
+                pool1.at[pl.ds(pl.multiple_of(me * 8, 8), 8)],
+                spread_sem.at[0, k - 1],
+                spread_sem.at[1, k - 1],
                 friends[k - 1],
             )
         )
-    states_ref[:, rows, :] = stage[me]
+    next_hop(0, 1)
+    own.wait()
+    for copy in pieces:
+        copy.wait_recv()
+    first_hop(1, pool1)
+    next_hop(0, 2)
+    next_hop(0, 3)
+    next_hop(1, 1)
+    hand_out(0)
+    next_hop(1, 2)
+    next_hop(1, 3)
+    hand_out(1)
     for copy in hands:
         copy.wait_recv()
-    for copy in hands + list(copies.values()):
+    for copy in hands + pieces + list(copies.values()):
         copy.wait_send()
 
 
-def gather(caps, chunk, number, order, loc, pool):
+def gather(caps, chunk, number, order, loc, pool, enc):
     total = sum(caps)
     return pl.pallas_call(
         functools.partial(gather_kernel, caps, chunk),
@@ -333,20 +390,26 @@
             pl.BlockSpec(memory_space=pltpu.SMEM),
             pl.BlockSpec(memory_space=pltpu.SMEM),
             pl.BlockSpec(memory_space=pltpu.VMEM),
+            pl.BlockSpec(memory_space=pl.ANY),
         ],
         out_specs=pl.BlockSpec(memory_space=pltpu.VMEM),
         out_shape=jax.ShapeDtypeStruct((4, 128, 512), BF),
         scratch_shapes=[
-            pltpu.VMEM((2, caps[0], 16, 512), BF),
-            pltpu.VMEM((2 * total + 64, 16, 512), BF),
-            pltpu.VMEM((8, 4, 16, 512), BF),
-            pltpu.SemaphoreType.DMA((2, 2, total // chunk)),
+            pltpu.VMEM((64, 16, 256), BF),
+            pltpu.VMEM((2, 2, caps[0], 16, 256), BF),
+            pltpu.VMEM((2 * total + 64, 16, 256), BF),
+            pltpu.VMEM((2 * total + 64, 16, 256), BF),
+            pltpu.VMEM((8, 4, 16, 256), BF),
+            pltpu.VMEM((8, 4, 16, 256), BF),
+            pltpu.SemaphoreType.DMA((2, 2, 2, total // chunk)),
+            pltpu.SemaphoreType.DMA((2, 2, 7)),
             pltpu.SemaphoreType.DMA((2, 7)),
+            pltpu.SemaphoreType.DMA,
         ],
         compiler_params=pltpu.CompilerParams(
             collective_id=number, has_side_effects=True, vmem_limit_bytes=24 * 2**20
         ),
-    )(order, loc, pool)
+    )(order, loc, pool, enc)
 
 
 def finish_kernel(
@@ -359,10 +422,13 @@
     dw_ref,
     gs_ref,
     gw_ref,
-    taken,
-    comb,
+    taken0,
+    taken1,
+    comb0,
+    comb1,
     outb,
-    inb,
+    inb0,
+    inb1,
     done,
     pair_in,
     held,
@@ -393,74 +459,127 @@
     def send(src, dst, sems, slot, target):
         return push(src, dst, sems.at[0, slot], sems.at[1, slot], target)
 
+    takens = (taken0, taken1)
+    combs = (comb0, comb1)
+    inbs = (inb0, inb1)
     given = []
-    for k in range(1, 8):
-        member = (me + k) % 8
-        given.append(
-            send(
-                ge_ref.at[:, pl.ds(pl.multiple_of(member * 16, 16), 16), :],
-                taken.at[pl.ds(me * 4, 4)],
-                team_sem,
-                k - 1,
-                friends[k - 1],
+
+    def give(h):
+        for k in range(1, 8):
+            member = (me + k) % 8
+            given.append(
+                push(
+                    ge_ref.at[
+                        :, pl.ds(pl.multiple_of(member * 16, 16), 16), pl.ds(h * 256, 256)
+                    ],
+                    takens[h].at[pl.ds(me * 4, 4)],
+                    team_sem.at[0, h, k - 1],
+                    team_sem.at[1, h, k - 1],
+                    friends[k - 1],
+                )
             )
-        )
+
+    give(0)
     offsets = (2, 1, 3, 0)
     partner = at(z, x, y, 1 - core)
     swaps = []
     for slot, offset in enumerate(offsets):
         theirs = (y + offset) % 4 * 2 + 1 - core
         swaps.append(send(dw_ref.at[theirs], pair_in.at[slot], core_sem, slot, partner))
-    taken[pl.ds(me * 4, 4)] = ge_ref[:, pl.ds(pl.multiple_of(me * 16, 16), 16), :]
-    taken[32] = jnp.zeros((16, 512), BF)
-    comb[32] = jnp.zeros((16, 512), F32)
-    inb[2 * total] = jnp.zeros((16, 512), BF)
-    for copy in given:
-        copy.wait_recv()
-
-    def combine(i, carry):
-        row = taken[mate_ref[i, 0]].astype(F32)
-        for t in range(1, 4):
-            row = row + taken[mate_ref[i, t]].astype(F32)
-        comb[i] = row
-        return carry
-
-    lax.fori_loop(0, 32, combine, 0)
+    give(1)
+
+    def combine(h):
+        taken, comb = takens[h], combs[h]
+        mine = pl.ds(pl.multiple_of(me * 16, 16), 16)
+        taken[pl.ds(me * 4, 4)] = ge_ref[:, mine, h * 256 : h * 256 + 256]
+        taken[32] = jnp.zeros((16, 256), BF)
+        comb[32] = jnp.zeros((16, 256), F32)
+        inbs[h][2 * total] = jnp.zeros((16, 256), BF)
+        for copy in given[h * 7 : h * 7 + 7]:
+            copy.wait_recv()
+
+        def step(i, carry):
+            row = taken[mate_ref[i, 0]].astype(F32)
+            for t in range(1, 4):
+                row = row + taken[mate_ref[i, t]].astype(F32)
+            comb[i] = row
+            return carry
+
+        lax.fori_loop(0, 32, step, 0, unroll=4)
+
     copies = {}
 
-    def back(r, i, added):
+    def back(h, r, i, added):
+        comb, inb = combs[h], inbs[h]
         for d in range(2):
             slot = d * total + first[r] + i * chunk
             if added:
-                copies[d, r + 1, i].wait_recv()
+                copies[h, d, r + 1, i].wait_recv()
                 further = d * total + first[r + 1] + i * chunk
 
                 def fill(j, carry, d=d, slot=slot, further=further):
-                    outb[slot + j] = (
+                    outb[h, slot + j] = (
                         comb[con_ref[d, r, i * chunk + j]] + inb[further + j].astype(F32)
                     ).astype(BF)
                     return carry
             else:
 
                 def fill(j, carry, d=d, slot=slot):
-                    outb[slot + j] = comb[con_ref[d, r, i * chunk + j]].astype(BF)
+                    outb[h, slot + j] = comb[con_ref[d, r, i * chunk + j]].astype(BF)
                     return carry
 
-            lax.fori_loop(0, chunk, fill, 0)
+            lax.fori_loop(0, chunk, fill, 0, unroll=4)
             index = (first[r] + i * chunk) // chunk
-            copies[d, r, i] = push(
-                outb.at[pl.ds(slot, chunk)],
+            copies[h, d, r, i] = push(
+                outb.at[h, pl.ds(slot, chunk)],
                 inb.at[pl.ds(slot, chunk)],
-                ring_sem.at[0, d, index],
-                ring_sem.at[1, d, index],
+                ring_sem.at[0, h, d, index],
+                ring_sem.at[1, h, d, index],
                 behind if d == 0 else ahead,
             )
 
-    for i in range(caps[3] // chunk):
-        back(3, i, False)
-    for r in (2, 1, 0):
-        for i in range(caps[r + 1] // chunk, caps[r] // chunk):
-            back(r, i, False)
+    def farthest(h):
+        for i in range(caps[3] // chunk):
+            back(h, 3, i, False)
+        for r in (2, 1, 0):
+            for i in range(caps[r + 1] // chunk, caps[r] // chunk):
+                back(h, r, i, False)
+
+    def nearer(h, r):
+        for i in range(caps[r + 1] // chunk):
+            back(h, r, i, True)
+
+    rows = pl.ds(pl.multiple_of(me * 16, 16), 16)
+    homes = []
+
+    def go_home(h):
+        comb, inb = combs[h], inbs[h]
+        for i in range(caps[0] // chunk):
+            for d in range(2):
+                copies[h, d, 0, i].wait_recv()
+
+        def close(i, carry):
+            for k in range(8):
+                b = i * 8 + k
+                done[h, i, k] = (
+                    inb[fin_ref[b, 0]].astype(F32)
+                    + inb[fin_ref[b, 1]].astype(F32)
+                    + comb[fin_ref[b, 2]]
+                ).astype(BF)
+            return carry
+
+        lax.fori_loop(0, 8, close, 0)
+        for k in range(1, 8):
+            homes.append(
+                push(
+                    done.at[h, (me + k) % 8],
+                    gs_ref.at[:, rows, pl.ds(h * 256, 256)],
+                    home_sem.at[0, h, k - 1],
+                    home_sem.at[1, h, k - 1],
+                    friends[k - 1],
+                )
+            )
+        gs_ref[:, rows, h * 256 : h * 256 + 256] = done[h, me]
 
     def add_pair(slot, offset):
         swaps[slot].wait_recv()
@@ -470,16 +589,19 @@
                 dw_ref[mine, part].astype(F32) + pair_in[slot, part].astype(F32)
             ).astype(BF)
 
+    combine(0)
+    farthest(0)
     add_pair(0, 2)
     up = send(held.at[0, pl.ds(0, 2)], y_half.at[0], y_sem, 0, sides[0])
     down = send(held.at[0, pl.ds(2, 2)], y_half.at[1], y_sem, 1, sides[1])
-    for i in range(caps[3] // chunk):
-        back(2, i, True)
+    nearer(0, 2)
+    combine(1)
+    farthest(1)
     add_pair(1, 1)
+    nearer(0, 1)
     add_pair(2, 3)
     add_pair(3, 0)
-    for i in range(caps[2] // chunk):
-        back(1, i, True)
+    nearer(0, 0)
     up.wait_recv()
     for part in range(2):
         held[1, part] = (held[1, part].astype(F32) + y_half[0, part].astype(F32)).astype(BF)
@@ -490,36 +612,9 @@
             held[2, part + 2].astype(F32) + y_half[1, part].astype(F32)
         ).astype(BF)
     down2 = send(held.at[2], y_in.at[1], y_sem, 3, sides[1])
-    for i in range(caps[1] // chunk):
-        back(0, i, True)
-    for i in range(caps[0] // chunk):
-        for d in range(2):
-            copies[d, 0, i].wait_recv()
-
-    def close(i, carry):
-        for k in range(8):
-            b = i * 8 + k
-            done[i, k] = (
-                inb[fin_ref[b, 0]].astype(F32)
-                + inb[fin_ref[b, 1]].astype(F32)
-                + comb[fin_ref[b, 2]]
-            ).astype(BF)
-        return carry
-
-    lax.fori_loop(0, 8, close, 0)
-    rows = pl.ds(pl.multiple_of(me * 16, 16), 16)
-    homes = []
-    for k in range(1, 8):
-        homes.append(
-            send(
-                done.at[(me + k) % 8],
-                gs_ref.at[:, rows, :],
-                home_sem,
-                k - 1,
-                friends[k - 1],
-            )
-        )
-    gs_ref[:, rows, :] = done[me]
+    nearer(1, 2)
+    go_home(0)
+    nearer(1, 1)
     up2.wait_recv()
     down2.wait_recv()
 
@@ -539,6 +634,7 @@
     ahead_x = y_total(1)
     behind_x = y_total(3)
     own = y_total(0)
+    nearer(1, 0)
     xup.wait_recv()
     held[4, 1, 0] = (ahead_x[0] + x_half[0].astype(F32)).astype(BF)
     held[4, 1, 1] = ahead_x[1].astype(BF)
@@ -557,6 +653,7 @@
         zs.append(
             send(held.at[4, 3, :, target], z_in.at[step - 1], z_sem, step - 1, around[step - 1])
         )
+    go_home(1)
     result = held[4, 3, :, z].astype(F32)
     for copy, step in zip(zs, (4, 3, 5, 2, 6, 1, 7)):
         copy.wait_recv()
@@ -582,11 +679,14 @@
             jax.ShapeDtypeStruct((2, 16, 256), F32),
         ],
         scratch_shapes=[
-            pltpu.VMEM((33, 16, 512), BF),
-            pltpu.VMEM((33, 16, 512), F32),
-            pltpu.VMEM((2 * total, 16, 512), BF),
-            pltpu.VMEM((2 * total + 1, 16, 512), BF),
-            pltpu.VMEM((8, 8, 16, 512), BF),
+            pltpu.VMEM((33, 16, 256), BF),
+            pltpu.VMEM((33, 16, 256), BF),
+            pltpu.VMEM((33, 16, 256), F32),
+            pltpu.VMEM((33, 16, 256), F32),
+            pltpu.VMEM((2, 2 * total, 16, 256), BF),
+            pltpu.VMEM((2 * total + 1, 16, 256), BF),
+            pltpu.VMEM((2 * total + 1, 16, 256), BF),
+            pltpu.VMEM((2, 8, 8, 16, 256), BF),
             pltpu.VMEM((4, 4, 2, 8, 16, 256), BF),
             pltpu.VMEM((5, 4, 2, 8, 16, 256), BF),
             pltpu.VMEM((2, 2, 2, 8, 16, 256), BF),
@@ -594,9 +694,9 @@
             pltpu.VMEM((2, 8, 16, 256), BF),
             pltpu.VMEM((2, 2, 8, 16, 256), BF),
             pltpu.VMEM((7, 2, 16, 256), BF),
-            pltpu.SemaphoreType.DMA((2, 7)),
-            pltpu.SemaphoreType.DMA((2, 2, total // chunk)),
-            pltpu.SemaphoreType.DMA((2, 7)),
+            pltpu.SemaphoreType.DMA((2, 2, 7)),
+            pltpu.SemaphoreType.DMA((2, 2, 2, total // chunk)),
+            pltpu.SemaphoreType.DMA((2, 2, 7)),
             pltpu.SemaphoreType.DMA((2, 4)),
             pltpu.SemaphoreType.DMA((2, 4)),
             pltpu.SemaphoreType.DMA((2, 4)),
@@ -633,14 +733,13 @@
     up = far(wanted[:, 1], wanted[:, 2], wanted[:, 3], wanted[:, 4] & even)
     down = far(wanted[:, 7], wanted[:, 6], wanted[:, 5], wanted[:, 4] & ~even)
     fars = jnp.stack([up, down], axis=1).astype(i32)
-    lengths = jnp.stack(
-        [jnp.max(jnp.sum((fars >= r).astype(i32), axis=-1)) for r in range(1, 5)]
-    )
-    fits = jnp.all(lengths <= jnp.array(TIGHT, i32))
+    reach = jnp.arange(1, 5, dtype=i32)[:, None, None, None, None]
+    lengths = jnp.sum((fars[None] >= reach).astype(i32), axis=-1)
+    fits = jnp.all(lengths <= jnp.array(TIGHT, i32)[:, None, None, None])
     fars = lax.dynamic_index_in_dim(fars, y, 0, keepdims=False)
     fars = lax.dynamic_slice_in_dim(jnp.concatenate([fars, fars], axis=1), z, 8, axis=1)
     key = fars * 64 + 63 - team
-    rank = jnp.sum((key[..., None, :] > key[..., :, None]).astype(i32), axis=-1)
+    rank = jnp.sum((key[..., :, None] > key[..., None, :]).astype(i32), axis=-2)
     at_rank = rank[..., None, :] == team[:, None]
     order = jnp.sum(jnp.where(at_rank[:, 0], team, 0), axis=-1)
 
@@ -705,11 +804,11 @@
     row = jnp.pad(neighbour_ids.reshape(1, 4), ((0, 0), (0, 124)))
     pool, ids = spread(row, enc_states[0])
     fits, order, mate, con, locate, collect = plan(ids[:, :, :, 0, :4])
-    pool = pool.reshape(64, 16, 512)
+    pool = pool.reshape(64, 16, 256)
     states = lax.cond(
         fits,
-        lambda: gather(TIGHT, 4, 2, order, locate(TIGHT), pool),
-        lambda: gather(WIDE, 16, 3, order, locate(WIDE), pool),
+        lambda: gather(TIGHT, 4, 2, order, locate(TIGHT), pool, enc_states[0]),
+        lambda: gather(WIDE, 16, 3, order, locate(WIDE), pool, enc_states[0]),
     )
     gq, grad_e, dw = attention(states.reshape(512, 512), kv_weight, queries[0], grad_out[0])
     grad_e = grad_e.reshape(4, 128, 512)

time: 167 us -> 147 us (0.88)
  Pallas kernels: 147 us -> 136 us
  other arithmetic: 10.6 us -> 5.16 us
  local copies, waits for them, and re-layouts: 7.04 us -> 3.72 us
    pallas_call x1, Pallas kernels: 64.6 us -> 57.4 us  [finish(): pl.pallas_call(functools.partial(finish_kernel, caps, chunk), in_specs=[s...]
    unnamed x10 -> x4, local copies, waits for them, and re-layouts: 5 us -> 1.59 us
    reduce_max x4 -> x0, other arithmetic: 2.63 us -> none  [plan(): jnp.max(jnp.sum((fars >= r).astype(i32), axis=-1))]
    reduce_and x1, other arithmetic: 3.99 us -> 1.38 us  [plan(): fits = jnp.all(lengths <= jnp.array(TIGHT, i32)[:, None, None, None])]
    pallas_call x1, Pallas kernels: 23.2 us -> 21 us  [spread(): pl.pallas_call(spread_kernel, in_specs=[pl.BlockSpec(memory_space=pltpu.V...]
where the time goes in v3:
time: 147 us
  Pallas kernels  136 us (93%)
  other arithmetic  5.16 us (4%)
  local copies, waits for them, and re-layouts  3.72 us (3%)
  between operations  1.56 us (1%)
    pallas_call x1, Pallas kernels, finish(): pl.pallas_call(functools.partial(finish_kernel, caps, chunk), in_specs=[s...  57.4 us
    pallas_call x1, Pallas kernels, gather(): pl.pallas_call(functools.partial(gather_kernel, caps, chunk), in_specs=[p...  39.5 us
    pallas_call x1, Pallas kernels, spread(): pl.pallas_call(spread_kernel, in_specs=[pl.BlockSpec(memory_space=pltpu.V...  21 us
    pallas_call x1, Pallas kernels, attention(): pl.pallas_call(attention_kernel, grid=(8,), in_specs=[pl.BlockSpec((keys,...  18.1 us

profile of v3, /device:TPU:1, one launch (start us, length us, event | category | flops | bytes accessed | tf_op | source)
XLA Modules:
  0.0 146.9 jit_solution(16266970297829196346)
XLA Ops:
  0.6 0.0 copy-start
  0.7 0.8 reshape.440
  1.6 0.1 add.309
  1.6 0.1 add.310
  1.8 0.1 sub.82
  1.9 21.0 %shard_map.85 = (bf16[8,8,16,256]{3,2,1,0:T(8,128)(2,1)S(1)}, s32[4,8,8,1,128]{4,3,2,1,0:T(1,128)S(1)}) custom-call(s32[1,128]{1,0:T(1,128)S(1)} %pad.4.row_ref, bf16[8,128,512]{2,1,0:T(8,128)(2,1)} %bitcast.105), custom_call_target="tpu_custom_call" | custom-call | tf_op jit(solution)/shard_map/pallas_call | solution.py:223
  22.9 0.4 fusion.44
  23.3 0.1 squeeze.84
  23.5 0.5 fusion.13
  23.9 0.1 reshape.441
  24.1 0.7 convert_reduce_fusion.1
  24.8 1.4 fusion.21
  26.9 0.2 convert_reduce_fusion
  27.1 0.1 broadcast_in_dim.230
  27.2 0.1 iota_compare_fusion.4
  27.4 0.2 broadcast_compare_fusion.2
  27.6 0.1 negate_select_fusion.3
  27.8 0.1 add_select_fusion.4
  27.8 0.1 reshape.442
  27.9 0.1 reshape.443
  28.0 0.1 select_reduce_fusion.7
  28.1 0.1 broadcast_compare_fusion.4
  28.2 0.1 slice_bitcast_fusion.17
  28.3 0.1 iota_compare_fusion.5
  28.4 0.1 select_reduce_fusion.6
  28.5 0.0 copy-done
  28.5 39.6 %conditional.2 = (bf16[512,512]{1,0:T(8,128)(2,1)S(1)}) conditional(s32[]{:T(128)} %convert_element_type.16, (pred[2,8,64,64]{3,2,1,0:T(8,128)(4,1)S(1)}, s32[2,64,64]{2,1,0:T(8,128)S(1)}, s32[32]{0:T(128)S(1)}, s32[32]{0:T(128)S(1)}, pred[32]{0:T(512)(128)(4,1)S(1)}, /*index=5*/s32[2,32]{1,0:T(2,128)S(1)}, bf16[8,8,16,256]{3,2,1,0:T(8,128)(2,1)S(1)}, ...), branch_computations={%region_4.6_spmd, %region_6.8_spmd} | conditional | flops 16800 | bytes 83112 | solution.py:808
  28.6 0.1 select_reduce_fusion.1.order_ref
  28.7 39.5 %branch_1_fun.4 = bf16[4,128,512]{2,1,0:T(8,128)(2,1)S(1)} custom-call(s32[2,64]{1,0:T(2,128)S(1)} %select_reduce_fusion.1.order_ref, s32[32]{0:T(128)S(1)} %compare_select_fusion.7.loc_ref, bf16[64,16,256]{2,1,0:T(8,128)(2,1)S(1)} %bitcast.109, bf16[8,128,512]{2,1,0:T(8,128)(2,1)S(1)} %bitcast.107), custom_call_target="tpu_custom_call" | custom-call | tf_op jit(solution)/shard_map/cond/branch_1_fun/pallas_call | solution.py:387
  68.2 0.1 and_convert_fusion
  68.2 18.1 %shard_map.86 = (bf16[128,2048]{1,0:T(8,128)(2,1)}, bf16[512,512]{1,0:T(8,128)(2,1)S(1)}, bf16[8,4,2,8,16,256]{5,4,3,2,1,0:T(8,128)(2,1)}) custom-call(bf16[512,512]{1,0:T(8,128)(2,1)S(1)} %get-tuple-element.550.states_ref, bf16[2,512,2048]{2,1,0:T(8,128)(2,1)} %w_ref.1, bf16[128,2048]{1,0:T(8,128)(2,1)} %bitcast.118, bf16[128,2048]{1,0:T(8,128)(2,1)} %bitcast.119), custom_call_target="tpu_custom_call" | custom-call | flops 7200000000 | bytes 12000000 | tf_op jit(solution)/shard_map/pallas_call | solution.py:91
  86.4 59.0 %conditional.3 = (f32[2,16,256]{2,1,0:T(8,128)S(1)}, bf16[1,8,128,512]{3,2,1,0:T(8,128)(2,1)S(1)}) conditional(s32[]{:T(128)} %convert_element_type.16, (pred[32,32]{1,0:T(8,128)(4,1)S(1)}, s32[32,32,32]{2,1,0:T(8,128)S(1)}, s32[32,4,32]{2,1,0:T(4,128)S(1)}, s32[32]{0:T(128)S(1)}, s32[2,4,1,64]{3,1,2,0:T(4,128)S(1)}, ...), branch_computations={%region_9.13_spmd, %region_13.17_spmd} | conditional | flops 114912 | bytes 208788 | solution.py:815
  86.4 0.2 select_reduce_fusion.4
  86.6 0.6 reduce_sum.93
  87.3 0.6 select_reduce_fusion.5
  87.9 0.1 copy.45.fin_ref
  88.0 57.4 %branch_1_fun.5 = (bf16[8,128,512]{2,1,0:T(8,128)(2,1)S(1)}, f32[2,16,256]{2,1,0:T(8,128)S(1)}) custom-call(s32[32,4]{1,0:T(8,128)S(1)} %broadcast_add_fusion.4.mate_ref, s32[2,4,64]{2,1,0:T(4,128)S(1)} %broadcast_add_fusion.6.con_ref, s32[64,3]{1,0:T(8,128)S(1)} %copy.45.fin_ref, bf16[4,128,512]{2,1,0:T(8,128)(2,1)S(1)} %bitcast.111, ...), custom_call_target="tpu_custom_call" | custom-call | tf_op jit(solution)/shard_map/cond/branch_1_fun/pallas_call | solution.py:673
  145.4 1.0 copy.64
  146.3 0.6 copy.65
  (32 shorter events, 0.4 us)
Async XLA Ops:
  0.6 27.9 %copy-start = (bf16[1,8,128,512]{3,2,1,0:T(8,128)(2,1)S(1)}, bf16[1,8,128,512]{3,2,1,0:T(8,128)(2,1)}, u32[]{:S(2)}) copy-start(bf16[1,8,128,512]{3,2,1,0:T(8,128)(2,1)} %param.12) | copy-start | bytes 3145732

commit v4 on v3

v4 whole, which is shorter than its diff:
```python
import functools
import math

import jax
import jax.numpy as jnp
from jax import lax
from jax.experimental import pallas as pl
from jax.experimental.pallas import tpu as pltpu
from jax.sharding import PartitionSpec as P

DH = 128
BF = jnp.bfloat16
F32 = jnp.float32
MESH = pl.DeviceIdType.MESH
NT = (((1,), (1,)), ((), ()))
TN = (((0,), (0,)), ((), ()))


def place():
    seq = lax.axis_index("seq")
    grp = lax.axis_index("grp")
    return seq // 4, seq % 4, grp // 2, grp % 2


def at(z, x, y, core):
    return {"seq": (z + 8) % 8 * 4 + (x + 4) % 4, "grp": (y + 4) % 4 * 2 + core}


def teammate(z, y, member):
    return at(z, member // 2, y, member % 2)


def greet(friends):
    barrier = pltpu.get_barrier_semaphore()
    for friend in friends:
        pl.semaphore_signal(barrier, inc=1, device_id=friend, device_id_type=MESH)
    pl.semaphore_wait(barrier, len(friends))


def push(src, dst, send_sem, recv_sem, target):
    copy = pltpu.make_async_remote_copy(
        src_ref=src,
        dst_ref=dst,
        send_sem=send_sem,
        recv_sem=recv_sem,
        device_id=target,
        device_id_type=MESH,
    )
    copy.start()
    return copy


def head_pair(step, y, core):
    return (y + 6 - step // 2) % 4 * 2 + (core + 1 + step % 2) % 2


def attention_kernel(
    states_ref,
    w_ref,
    q_ref,
    go_ref,
    gq_ref,
    ge_ref,
    sums_ref,
    st_ref,
    acc_ref,
    pair_out,
    pair_in,
    far_out,
    y_half,
    core_sem,
    y_sem,
):
    step = pl.program_id(0)
    z, x, y, core = place()
    other = at(z, x, y, 1 - core)
    sides = [at(z, x, y + 1, core), at(z, x, y - 1, core)]
    scale = 1.0 / math.sqrt(DH)

    @pl.when(step == 0)
    def _():
        st_ref[...] = states_ref[...].T
        acc_ref[...] = jnp.zeros_like(acc_ref)
        barrier = pltpu.get_barrier_semaphore()
        for friend in [other] + sides:
            pl.semaphore_signal(barrier, inc=1, device_id=friend, device_id_type=MESH)

    states = states_ref[...]
    wk = w_ref[0]
    wv = w_ref[1]
    keys = jnp.dot(states, wk, preferred_element_type=F32).astype(BF)
    values = jnp.dot(states, wv, preferred_element_type=F32).astype(BF)
    blank = jnp.zeros((64, DH), BF)
    gk_parts = []
    gv_parts = []
    for span in range(2):
        q = q_ref[span * 64 : span * 64 + 64, :]
        go = go_ref[span * 64 : span * 64 + 64, :]
        key = keys[span * 256 : span * 256 + 256, :]
        value = values[span * 256 : span * 256 + 256, :]
        qd = jnp.concatenate(
            [
                jnp.concatenate([q[:, :DH], blank], axis=1),
                jnp.concatenate([blank, q[:, DH:]], axis=1),
            ],
            axis=0,
        )
        gd = jnp.concatenate(
            [
                jnp.concatenate([go[:, :DH], blank], axis=1),
                jnp.concatenate([blank, go[:, DH:]], axis=1),
            ],
            axis=0,
        )
        scores = lax.dot_general(key, qd, NT, preferred_element_type=F32) * scale
        top = jnp.max(scores, axis=0, keepdims=True)
        expo = jnp.exp(scores - top)
        weights = expo / jnp.sum(expo, axis=0, keepdims=True)
        weights_b = weights.astype(BF)
        gp = lax.dot_general(value, gd, NT, preferred_element_type=F32)
        delta = jnp.sum(weights_b.astype(F32) * gp, axis=0, keepdims=True)
        gs = (weights * (gp - delta) * scale).astype(BF)
        gv_parts.append(jnp.dot(weights_b, gd, preferred_element_type=F32).astype(BF))
        gk_parts.append(jnp.dot(gs, qd, preferred_element_type=F32).astype(BF))
        gq = lax.dot_general(gs, key, TN, preferred_element_type=F32).astype(BF)
        gq_ref[span * 64 : span * 64 + 64, :DH] = gq[:64, :DH]
        gq_ref[span * 64 : span * 64 + 64, DH:] = gq[64:, DH:]
    gk = jnp.concatenate(gk_parts, axis=0)
    gv = jnp.concatenate(gv_parts, axis=0)
    total = acc_ref[...]
    total = total + lax.dot_general(gk, wk, NT, preferred_element_type=F32)
    total = total + lax.dot_general(gv, wv, NT, preferred_element_type=F32)
    acc_ref[...] = total

    @pl.when(step == pl.num_programs(0) - 1)
    def _():
        ge_ref[...] = total.astype(BF)

    turned = st_ref[...]
    shares = [jnp.dot(turned, part, preferred_element_type=F32) for part in (gk, gv)]
    slot = step // 2

    def swap(k):
        return pltpu.make_async_remote_copy(
            src_ref=pair_out.at[k],
            dst_ref=pair_in.at[k],
            send_sem=core_sem.at[0, k],
            recv_sem=core_sem.at[1, k],
            device_id=other,
            device_id_type=MESH,
        )

    def opposite(side):
        return pltpu.make_async_remote_copy(
            src_ref=far_out.at[pl.ds(side * 2, 2)],
            dst_ref=y_half.at[side],
            send_sem=y_sem.at[0, side],
            recv_sem=y_sem.at[1, side],
            device_id=sides[side],
            device_id_type=MESH,
        )

    def each(write):
        for kind in range(2):
            for zz in range(8):
                for xx in range(4):
                    row = (zz * 4 + xx) * 16
                    write(xx, kind, zz, shares[kind][row : row + 16, :])

    @pl.when(step % 2 == 0)
    def _():
        def write(xx, kind, zz, part):
            pair_out[slot, xx, kind, zz] = part.astype(BF)

        each(write)

        @pl.when(step == 0)
        def _():
            pl.semaphore_wait(pltpu.get_barrier_semaphore(), 3)

        swap(slot).start()

    @pl.when(step % 2 == 1)
    def _():
        swap(slot).wait_recv()

        @pl.when(step == 1)
        def _():
            def write(xx, kind, zz, part):
                far_out[xx, kind, zz] = (part + pair_in[0, xx, kind, zz].astype(F32)).astype(BF)

            each(write)
            for side in range(2):
                opposite(side).start()

        @pl.when(step > 1)
        def _():
            def write(xx, kind, zz, part):
                sums_ref[slot - 1, xx, kind, zz] = (
                    part + pair_in[slot, xx, kind, zz].astype(F32)
                ).astype(BF)

            each(write)

        @pl.when(step == 7)
        def _():
            opposite(0).wait_recv()
            for part in range(2):
                sums_ref[0, part] = (
                    sums_ref[0, part].astype(F32) + y_half[0, part].astype(F32)
                ).astype(BF)
            opposite(1).wait_recv()
            for part in range(2):
                sums_ref[2, part + 2] = (
                    sums_ref[2, part + 2].astype(F32) + y_half[1, part].astype(F32)
                ).astype(BF)
            for side in range(2):
                opposite(side).wait_send()
            for k in range(4):
                swap(k).wait_send()


def attention(states, weights, queries, grad_out):
    keys, enc = states.shape
    tokens, width = queries.shape

    def columns(i):
        _, _, y, core = place()
        return head_pair(i, y, core)

    return pl.pallas_call(
        attention_kernel,
        grid=(8,),
        in_specs=[
            pl.BlockSpec((keys, enc), lambda i: (0, 0)),
            pl.BlockSpec((2, enc, 256), lambda i: (0, 0, columns(i))),
            pl.BlockSpec((tokens, 256), lambda i: (0, columns(i))),
            pl.BlockSpec((tokens, 256), lambda i: (0, columns(i))),
        ],
        out_specs=[
            pl.BlockSpec((tokens, 256), lambda i: (0, columns(i))),
            pl.BlockSpec((keys, enc), lambda i: (0, 0)),
            pl.BlockSpec((3, 4, 2, 8, 16, 256), lambda i: (0, 0, 0, 0, 0, 0)),
        ],
        out_shape=[
            jax.ShapeDtypeStruct((tokens, width), BF),
            jax.ShapeDtypeStruct((keys, enc), BF),
            jax.ShapeDtypeStruct((3, 4, 2, 8, 16, 256), BF),
        ],
        scratch_shapes=[
            pltpu.VMEM((enc, keys), BF),
            pltpu.VMEM((keys, enc), F32),
            pltpu.VMEM((4, 4, 2, 8, 16, 256), BF),
            pltpu.VMEM((4, 4, 2, 8, 16, 256), BF),
            pltpu.VMEM((4, 2, 8, 16, 256), BF),
            pltpu.VMEM((2, 2, 2, 8, 16, 256), BF),
            pltpu.SemaphoreType.DMA((2, 4)),
            pltpu.SemaphoreType.DMA((2, 2)),
        ],
        compiler_params=pltpu.CompilerParams(
            collective_id=6, has_side_effects=True, vmem_limit_bytes=60 * 2**20
        ),
        cost_estimate=pl.CostEstimate(
            flops=7_200_000_000, bytes_accessed=12_000_000, transcendentals=600_000
        ),
    )(states, weights, queries, grad_out)


OUT = ((0, 256), (256, 128), (384, 128))
BACK = ((0, 128), (128, 256), (384, 128))


def piece(member):
    return pl.ds(pl.multiple_of(member * 16, 16), 16)


def spread_kernel(
    mine_ref, enc_ref, pool_ref, packed_ref, ids_ref, team_sem, xy_sem, zc_sem, own_sem
):
    z, x, y, core = place()
    me = x * 2 + core
    columns = pl.ds(*OUT[0])
    team = [teammate(z, y, (me + k) % 8) for k in range(1, 8)]
    flat = [at(z, x + k // 4, y + k % 4, core) for k in range(1, 16)]
    upright = [at(z + k // 2, x, y, (core + k % 2) % 2) for k in range(1, 16)]
    own = pltpu.make_async_copy(enc_ref.at[:, piece(me), columns], pool_ref.at[me], own_sem)
    own.start()
    lane = lax.broadcasted_iota(jnp.int32, (1, 128), 1) - (z % 4 * 32 + me * 4)
    line = jnp.zeros((1, 128), jnp.int32)
    for ref in range(4):
        line = jnp.where(lane == ref, mine_ref[0, ref // 2, ref % 2], line)
    ids_ref[z, core, x, y] = line
    greet(flat + upright + [at(z, x + k, y, 1 - core) for k in range(1, 4)])
    rows = []
    for k in range(1, 16):
        rows.append(
            push(
                ids_ref.at[z, core, x, y],
                ids_ref.at[z, core, x, y],
                xy_sem.at[0, k - 1],
                xy_sem.at[1, k - 1],
                flat[k - 1],
            )
        )
    pieces = []
    for k in range(1, 8):
        pieces.append(
            push(
                enc_ref.at[:, piece((me + k) % 8), columns],
                pool_ref.at[me],
                team_sem.at[0, k - 1],
                team_sem.at[1, k - 1],
                team[k - 1],
            )
        )
    for copy in rows:
        copy.wait_recv()
    planes = []
    for k in range(1, 16):
        planes.append(
            push(
                ids_ref.at[z, core],
                ids_ref.at[z, core],
                zc_sem.at[0, k - 1],
                zc_sem.at[1, k - 1],
                upright[k - 1],
            )
        )
    own.wait()
    for copy in planes + pieces:
        copy.wait_recv()
    for yy in range(4):
        for half in range(2):
            line = jnp.zeros((1, 128), jnp.int32)
            for zz in range(half * 4, half * 4 + 4):
                for cc in range(2):
                    for xx in range(4):
                        line = line + ids_ref[zz, cc, xx, yy]
            packed_ref[yy, half : half + 1, :] = line
    for copy in rows + pieces + planes:
        copy.wait_send()


def spread(mine, enc):
    return pl.pallas_call(
        spread_kernel,
        in_specs=[
            pl.BlockSpec(memory_space=pltpu.SMEM),
            pl.BlockSpec(memory_space=pl.ANY),
        ],
        out_specs=[
            pl.BlockSpec(memory_space=pltpu.VMEM),
            pl.BlockSpec(memory_space=pltpu.VMEM),
        ],
        out_shape=[
            jax.ShapeDtypeStruct((8, 8, 16, OUT[0][1]), BF),
            jax.ShapeDtypeStruct((4, 2, 128), jnp.int32),
        ],
        scratch_shapes=[
            pltpu.VMEM((8, 2, 4, 4, 1, 128), jnp.int32),
            pltpu.SemaphoreType.DMA((2, 7)),
            pltpu.SemaphoreType.DMA((2, 15)),
            pltpu.SemaphoreType.DMA((2, 15)),
            pltpu.SemaphoreType.DMA,
        ],
        compiler_params=pltpu.CompilerParams(
            collective_id=1, has_side_effects=True, vmem_limit_bytes=60 * 2**20
        ),
    )(mine, enc)


def starts(caps):
    return [0] + [sum(caps[: r + 1]) for r in range(len(caps))]


def chunks(marks, cap):
    ends = [mark for mark in marks if mark <= cap]
    return list(zip([0] + ends[:-1], ends))


def gather_kernel(caps, order_ref, loc_ref, pool_ref, enc_ref, states_ref, *scratch):
    count = len(OUT)
    pools = (pool_ref,) + scratch[: count - 1]
    packeds = scratch[count - 1 : 2 * count - 1]
    arrs = scratch[2 * count - 1 : 3 * count - 1]
    stages = scratch[3 * count - 1 : 4 * count - 1]
    ring_sem, team_sem, spread_sem, own_sem = scratch[4 * count - 1 :]
    z, x, y, core = place()
    me = x * 2 + core
    total = sum(caps)
    first = starts(caps)
    marks = sorted(set(caps))
    friends = [teammate(z, y, (me + k) % 8) for k in range(1, 8)]
    ahead = at(z + 1, x, y, core)
    behind = at(z - 1, x, y, core)
    owns = []
    for h in range(1, count):
        owns.append(
            pltpu.make_async_copy(
                enc_ref.at[:, piece(me), pl.ds(*OUT[h])], pools[h].at[me], own_sem.at[h - 1]
            )
        )
        owns[-1].start()
    greet(friends + [ahead, behind])
    copies = {}

    def forward(h, d, r, i, src, low, high):
        copies[h, d, r, i] = push(
            src,
            arrs[h].at[pl.ds(d * total + first[r] + low, high - low)],
            ring_sem.at[0, h, d, r, i],
            ring_sem.at[1, h, d, r, i],
            ahead if d == 0 else behind,
        )

    def first_hop(h):
        pool = pools[h]
        for i, (low, high) in enumerate(chunks(marks, caps[0])):
            for d in range(2):

                def fill(j, carry, d=d):
                    block = order_ref[d, j]
                    packeds[h][d, j] = pool[block // 8, block % 8]
                    return carry

                lax.fori_loop(low, high, fill, 0, unroll=2)
                forward(h, d, 0, i, packeds[h].at[d, pl.ds(low, high - low)], low, high)

        def keep(j, carry):
            for k in range(8):
                arrs[h][2 * total + j * 8 + k] = pool[j, k]
            return carry

        lax.fori_loop(0, 8, keep, 0)

    def next_hop(h, r):
        for i, (low, high) in enumerate(chunks(marks, caps[r])):
            for d in range(2):
                copies[h, d, r - 1, i].wait_recv()
                src = arrs[h].at[pl.ds(d * total + first[r - 1] + low, high - low)]
                forward(h, d, r, i, src, low, high)

    hands = []

    def hand_out(h):
        for r in range(4):
            done = len(chunks(marks, caps[r + 1])) if r < 3 else 0
            for i in range(done, len(chunks(marks, caps[r]))):
                for d in range(2):
                    copies[h, d, r, i].wait_recv()

        def pick(i, carry):
            for k in range(4):
                stages[h][i, k] = arrs[h][loc_ref[i * 4 + k]]
            return carry

        lax.fori_loop(0, 8, pick, 0)
        for k in range(1, 8):
            hands.append(
                push(
                    stages[h].at[(me + k) % 8],
                    states_ref.at[:, piece(me), pl.ds(*OUT[h])],
                    team_sem.at[0, h, k - 1],
                    team_sem.at[1, h, k - 1],
                    friends[k - 1],
                )
            )
        low, wide = OUT[h]
        states_ref[:, piece(me), low : low + wide] = stages[h][me]

    pieces = {}

    def more(h):
        for k in range(1, 8):
            pieces[h, k] = push(
                enc_ref.at[:, piece((me + k) % 8), pl.ds(*OUT[h])],
                pools[h].at[me],
                spread_sem.at[0, h - 1, k - 1],
                spread_sem.at[1, h - 1, k - 1],
                friends[k - 1],
            )

    def here(h):
        owns[h - 1].wait()
        for k in range(1, 8):
            pieces[h, k].wait_recv()

    more(1)
    more(2)
    first_hop(0)
    here(1)
    first_hop(1)
    next_hop(0, 1)
    here(2)
    first_hop(2)
    next_hop(1, 1)
    next_hop(0, 2)
    next_hop(2, 1)
    next_hop(1, 2)
    next_hop(0, 3)
    next_hop(2, 2)
    next_hop(1, 3)
    hand_out(0)
    next_hop(2, 3)
    hand_out(1)
    hand_out(2)
    for copy in hands:
        copy.wait_recv()
    for copy in hands + list(pieces.values()) + list(copies.values()):
        copy.wait_send()


def gather(caps, number, order, loc, pool, enc):
    total = sum(caps)
    count = len(OUT)
    return pl.pallas_call(
        functools.partial(gather_kernel, caps),
        in_specs=[
            pl.BlockSpec(memory_space=pltpu.SMEM),
            pl.BlockSpec(memory_space=pltpu.SMEM),
            pl.BlockSpec(memory_space=pltpu.VMEM),
            pl.BlockSpec(memory_space=pl.ANY),
        ],
        out_specs=pl.BlockSpec(memory_space=pltpu.VMEM),
        out_shape=jax.ShapeDtypeStruct((4, 128, 512), BF),
        scratch_shapes=[pltpu.VMEM((8, 8, 16, wide), BF) for _, wide in OUT[1:]]
        + [pltpu.VMEM((2, caps[0], 16, wide), BF) for _, wide in OUT]
        + [pltpu.VMEM((2 * total + 64, 16, wide), BF) for _, wide in OUT]
        + [pltpu.VMEM((8, 4, 16, wide), BF) for _, wide in OUT]
        + [
            pltpu.SemaphoreType.DMA((2, count, 2, 4, 4)),
            pltpu.SemaphoreType.DMA((2, count, 7)),
            pltpu.SemaphoreType.DMA((2, count - 1, 7)),
            pltpu.SemaphoreType.DMA((count - 1,)),
        ],
        compiler_params=pltpu.CompilerParams(
            collective_id=number, has_side_effects=True, vmem_limit_bytes=60 * 2**20
        ),
    )(order, loc, pool, enc)


def finish_kernel(
    caps,
    mate_ref,
    con_ref,
    fin_ref,
    ge_ref,
    sums_ref,
    gs_ref,
    gw_ref,
    *scratch,
):
    count = len(BACK)
    takens, combs, outbs, inbs, dones = (scratch[k * count : k * count + count] for k in range(5))
    held, y_in, x_half, x_in, z_in, team_sem, ring_sem, home_sem, y_sem, x_sem, z_sem = scratch[
        5 * count :
    ]
    z, x, y, core = place()
    me = x * 2 + core
    total = sum(caps)
    first = starts(caps)
    marks = sorted(set(caps))
    friends = [teammate(z, y, (me + k) % 8) for k in range(1, 8)]
    around = [at(z + k, x, y, core) for k in range(1, 8)]
    ahead = around[0]
    behind = around[6]
    sides = [at(z, x, y + 1, core), at(z, x, y - 1, core)]
    greet(friends + around + sides)

    def send(src, dst, sems, slot, target):
        return push(src, dst, sems.at[0, slot], sems.at[1, slot], target)

    given = []

    def give(h):
        for k in range(1, 8):
            given.append(
                push(
                    ge_ref.at[:, piece((me + k) % 8), pl.ds(*BACK[h])],
                    takens[h].at[pl.ds(me * 4, 4)],
                    team_sem.at[0, h, k - 1],
                    team_sem.at[1, h, k - 1],
                    friends[k - 1],
                )
            )

    give(0)
    up = send(sums_ref.at[0], y_in.at[0], y_sem, 0, sides[0])
    down = send(sums_ref.at[2], y_in.at[1], y_sem, 1, sides[1])
    give(1)
    give(2)

    def combine(h):
        taken, comb = takens[h], combs[h]
        low, wide = BACK[h]
        taken[pl.ds(me * 4, 4)] = ge_ref[:, piece(me), low : low + wide]
        taken[32] = jnp.zeros((16, wide), BF)
        comb[32] = jnp.zeros((16, wide), F32)
        inbs[h][2 * total] = jnp.zeros((16, wide), BF)
        for copy in given[h * 7 : h * 7 + 7]:
            copy.wait_recv()

        def step(i, carry):
            row = taken[mate_ref[0, i]].astype(F32)
            for t in range(1, 4):
                row = row + taken[mate_ref[t, i]].astype(F32)
            comb[i] = row
            return carry

        lax.fori_loop(0, 32, step, 0, unroll=4)

    copies = {}

    def back(h, r, i, added):
        comb, inb, outb = combs[h], inbs[h], outbs[h]
        low, high = chunks(marks, caps[r])[i]
        for d in range(2):
            base = d * total + first[r]
            if added:
                copies[h, d, r + 1, i].wait_recv()
                further = d * total + first[r + 1]

                def fill(j, carry, d=d, base=base, further=further):
                    outb[base + j] = (
                        comb[con_ref[d, r, j]] + inb[further + j].astype(F32)
                    ).astype(BF)
                    return carry
            else:

                def fill(j, carry, d=d, base=base):
                    outb[base + j] = comb[con_ref[d, r, j]].astype(BF)
                    return carry

            lax.fori_loop(low, high, fill, 0, unroll=2)
            copies[h, d, r, i] = push(
                outb.at[pl.ds(base + low, high - low)],
                inb.at[pl.ds(base + low, high - low)],
                ring_sem.at[0, h, d, r, i],
                ring_sem.at[1, h, d, r, i],
                behind if d == 0 else ahead,
            )

    def farthest(h):
        for i in range(len(chunks(marks, caps[3]))):
            back(h, 3, i, False)
        for r in (2, 1, 0):
            for i in range(len(chunks(marks, caps[r + 1])), len(chunks(marks, caps[r]))):
                back(h, r, i, False)

    def nearer(h, r):
        for i in range(len(chunks(marks, caps[r + 1]))):
            back(h, r, i, True)

    homes = []

    def go_home(h):
        comb, inb = combs[h], inbs[h]
        for i in range(len(chunks(marks, caps[0]))):
            for d in range(2):
                copies[h, d, 0, i].wait_recv()

        def close(i, carry):
            for k in range(8):
                b = i * 8 + k
                dones[h][i, k] = (
                    inb[fin_ref[0, b]].astype(F32)
                    + inb[fin_ref[1, b]].astype(F32)
                    + comb[fin_ref[2, b]]
                ).astype(BF)
            return carry

        lax.fori_loop(0, 8, close, 0)
        for k in range(1, 8):
            homes.append(
                push(
                    dones[h].at[(me + k) % 8],
                    gs_ref.at[:, piece(me), pl.ds(*BACK[h])],
                    home_sem.at[0, h, k - 1],
                    home_sem.at[1, h, k - 1],
                    friends[k - 1],
                )
            )
        low, wide = BACK[h]
        gs_ref[:, piece(me), low : low + wide] = dones[h][me]

    def y_total(offset):
        part = (x + offset) % 4
        return (
            sums_ref[1, part].astype(F32)
            + y_in[0, part].astype(F32)
            + y_in[1, part].astype(F32)
        )

    combine(0)
    farthest(0)
    combine(1)
    nearer(0, 2)
    farthest(1)
    nearer(0, 1)
    combine(2)
    nearer(1, 2)
    nearer(0, 0)
    farthest(2)
    left = at(z, x - 1, y, core)
    right = at(z, x + 1, y, core)
    up.wait_recv()
    down.wait_recv()
    held[0] = y_total(2).astype(BF)
    xup = send(held.at[0, 0], x_half.at[0], x_sem, 0, right)
    xdown = send(held.at[0, 1], x_half.at[1], x_sem, 1, left)
    nearer(1, 1)
    ahead_x = y_total(1)
    xup.wait_recv()
    held[1, 0] = (ahead_x[0] + x_half[0].astype(F32)).astype(BF)
    held[1, 1] = ahead_x[1].astype(BF)
    xup2 = send(held.at[1], x_in.at[0], x_sem, 2, right)
    behind_x = y_total(3)
    xdown.wait_recv()
    held[2, 0] = behind_x[0].astype(BF)
    held[2, 1] = (behind_x[1] + x_half[1].astype(F32)).astype(BF)
    xdown2 = send(held.at[2], x_in.at[1], x_sem, 3, left)
    go_home(0)
    nearer(2, 2)
    nearer(1, 0)
    xup2.wait_recv()
    xdown2.wait_recv()
    held[3] = (y_total(0) + x_in[0].astype(F32) + x_in[1].astype(F32)).astype(BF)
    zs = []
    for step in (4, 3, 5, 2, 6, 1, 7):
        target = (z + step) % 8
        zs.append(
            send(held.at[3, :, target], z_in.at[step - 1], z_sem, step - 1, around[step - 1])
        )
    nearer(2, 1)
    go_home(1)
    nearer(2, 0)
    go_home(2)
    result = held[3, :, z].astype(F32)
    for copy, step in zip(zs, (4, 3, 5, 2, 6, 1, 7)):
        copy.wait_recv()
        result = result + z_in[step - 1].astype(F32)
    gw_ref[...] = result
    for copy in homes:
        copy.wait_recv()
    rest = [up, down, xup, xdown, xup2, xdown2] + zs
    for copy in given + homes + rest + list(copies.values()):
        copy.wait_send()


def finish(caps, number, mate, con, fin, ge, sums):
    total = sum(caps)
    count = len(BACK)
    smem = pl.BlockSpec(memory_space=pltpu.SMEM)
    vmem = pl.BlockSpec(memory_space=pltpu.VMEM)
    return pl.pallas_call(
        functools.partial(finish_kernel, caps),
        in_specs=[smem, smem, smem, vmem, vmem],
        out_specs=[vmem, vmem],
        out_shape=[
            jax.ShapeDtypeStruct((8, 128, 512), BF),
            jax.ShapeDtypeStruct((2, 16, 256), F32),
        ],
        scratch_shapes=[pltpu.VMEM((33, 16, wide), BF) for _, wide in BACK]
        + [pltpu.VMEM((33, 16, wide), F32) for _, wide in BACK]
        + [pltpu.VMEM((2 * total, 16, wide), BF) for _, wide in BACK]
        + [pltpu.VMEM((2 * total + 1, 16, wide), BF) for _, wide in BACK]
        + [pltpu.VMEM((8, 8, 16, wide), BF) for _, wide in BACK]
        + [
            pltpu.VMEM((4, 2, 8, 16, 256), BF),
            pltpu.VMEM((2, 4, 2, 8, 16, 256), BF),
            pltpu.VMEM((2, 8, 16, 256), BF),
            pltpu.VMEM((2, 2, 8, 16, 256), BF),
            pltpu.VMEM((7, 2, 16, 256), BF),
            pltpu.SemaphoreType.DMA((2, count, 7)),
            pltpu.SemaphoreType.DMA((2, count, 2, 4, 4)),
            pltpu.SemaphoreType.DMA((2, count, 7)),
            pltpu.SemaphoreType.DMA((2, 2)),
            pltpu.SemaphoreType.DMA((2, 4)),
            pltpu.SemaphoreType.DMA((2, 7)),
        ],
        compiler_params=pltpu.CompilerParams(
            collective_id=number, has_side_effects=True, vmem_limit_bytes=48 * 2**20
        ),
    )(mate, con, fin, ge, sums)


TIGHT = (22, 18, 14, 6)
MIDDLE = (24, 20, 16, 8)
WIDE = (64, 64, 64, 32)
CAPS = (TIGHT, MIDDLE, WIDE)


def plan(ids):
    z, x, y, core = place()
    i32 = jnp.int32
    place_of = jnp.arange(256, dtype=i32)[None, :]
    block = (ids // 8 % 4 * 2 + place_of // 4 % 2) * 8 + ids % 8
    owner_z = ids // 32
    away = (place_of // 32 - owner_z + 8) % 8
    flat = owner_z * 64 + block
    is_block = (flat[:, None, :] == jnp.arange(512, dtype=i32)[None, :, None]).astype(BF)
    is_away = (away[:, None, :] == jnp.arange(8, dtype=i32)[None, :, None]).astype(BF)
    wanted = jnp.einsum("ydr,ybr->ydb", is_away, is_block, preferred_element_type=F32) > 0.5
    wanted = wanted.reshape(4, 8, 8, 64)
    team = jnp.arange(64, dtype=i32)
    even = team % 2 == 0

    def far(one, two, three, four):
        return jnp.where(four, 4, jnp.where(three, 3, jnp.where(two, 2, jnp.where(one, 1, 0))))

    up = far(wanted[:, 1], wanted[:, 2], wanted[:, 3], wanted[:, 4] & even)
    down = far(wanted[:, 7], wanted[:, 6], wanted[:, 5], wanted[:, 4] & ~even)
    fars = jnp.stack([up, down], axis=1).astype(i32)
    reach = jnp.arange(1, 5, dtype=i32)[:, None, None, None, None]
    lengths = jnp.sum((fars[None] >= reach).astype(i32), axis=-1)
    longest = jnp.max(lengths, axis=(1, 2, 3))
    level = jnp.where(
        jnp.all(longest <= jnp.array(TIGHT, i32)),
        0,
        jnp.where(jnp.all(longest <= jnp.array(MIDDLE, i32)), 1, 2),
    )
    fars = lax.dynamic_index_in_dim(fars, y, 0, keepdims=False)
    fars = lax.dynamic_slice_in_dim(jnp.concatenate([fars, fars], axis=1), z, 8, axis=1)
    key = fars * 64 + 63 - team
    rank = jnp.sum((key[..., :, None] > key[..., None, :]).astype(i32), axis=-2)
    at_rank = rank[..., :, None] == team
    order = jnp.sum(jnp.where(at_rank[:, 0], team[:, None], 0), axis=-2)

    def mine(a):
        return lax.dynamic_slice(a, (y, z * 32), (1, 32)).reshape(32)

    my_block, my_away = mine(block), mine(away)
    my_flat = (8 - my_away) % 8 * 64 + my_block
    upwards = (my_away < 4) | ((my_away == 4) & (my_block % 2 == 0))
    hops = jnp.where(upwards, my_away, 8 - my_away)
    hit = my_flat[:, None] == jnp.arange(512, dtype=i32)[None, :]
    ranks = lax.dot_general(
        rank.reshape(2, 512).astype(BF), hit.astype(BF), NT, preferred_element_type=F32
    ).astype(i32)
    spot = jnp.where(upwards, ranks[0], ranks[1])
    refs = jnp.arange(32, dtype=i32)
    first = jnp.min(jnp.where(hit, refs[:, None], 32), axis=0).reshape(8, 64)
    same = my_flat[:, None] == my_flat[None, :]
    earlier = jnp.sum(
        (same[None] & (refs[None, :, None] < refs[:, None, None])).astype(i32), axis=1
    )
    turns = jnp.arange(4, dtype=i32)[:, None, None]
    mate = 32 + jnp.sum(
        jnp.where(same[None] & (earlier[None] == turns), refs[:, None] - 32, 0), axis=1
    )
    firsts = jnp.stack(
        [
            jnp.stack([first[7], first[6], first[5], jnp.where(even, first[4], 32)]),
            jnp.stack([first[1], first[2], first[3], jnp.where(even, 32, first[4])]),
        ]
    )
    at_rank_by_hop = jnp.stack(
        [
            jnp.stack([at_rank[0, 7], at_rank[0, 6], at_rank[0, 5], at_rank[0, 4]]),
            jnp.stack([at_rank[1, 1], at_rank[1, 2], at_rank[1, 3], at_rank[1, 4]]),
        ]
    )
    con = 32 + jnp.sum(jnp.where(at_rank_by_hop, firsts[..., None] - 32, 0), axis=-2)

    def locate(caps):
        total = sum(caps)
        offset = sum(jnp.where(hops == r + 1, starts(caps)[r], 0) for r in range(4))
        there = jnp.where(upwards, 0, total) + offset + spot
        return jnp.where(my_away == 0, 2 * total + my_block, there)

    def collect(caps):
        total = sum(caps)
        return jnp.stack(
            [
                jnp.where(fars[0, 0] > 0, rank[0, 0], 2 * total),
                jnp.where(fars[1, 0] > 0, total + rank[1, 0], 2 * total),
                first[0],
            ]
        )

    return level, order, mate, con, locate, collect


def body(queries, grad_out, enc_states, neighbour_ids, kv_weight):
    enc = enc_states[0]
    pool, ids = spread(neighbour_ids, enc)
    level, order, mate, con, locate, collect = plan(ids.reshape(4, 256))
    states = lax.switch(
        level,
        [
            lambda caps=caps, number=number: gather(caps, number, order, locate(caps), pool, enc)
            for caps, number in zip(CAPS, (2, 3, 7))
        ],
    )
    gq, grad_e, sums = attention(states.reshape(512, 512), kv_weight, queries[0], grad_out[0])
    grad_e = grad_e.reshape(4, 128, 512)
    grad_states, grad_weight = lax.switch(
        level,
        [
            lambda caps=caps, number=number: finish(
                caps, number, mate, con, collect(caps), grad_e, sums
            )
            for caps, number in zip(CAPS, (4, 5, 8))
        ],
    )
    return (gq[None], grad_states[None], grad_weight)


def solution(mesh):
    placed = (
        P("grp", "seq", None),
        P("grp", "seq", None),
        P("grp", "seq", None, None),
        P("grp", "seq", None),
        P(),
    )
    return jax.shard_map(
        body,
        mesh=mesh,
        in_specs=placed,
        out_specs=(P("grp", "seq", None), P("grp", "seq", None, None), P(None, "seq", "grp")),
        check_vma=False,
    )
```

time: 147 us -> 139 us (0.946)
  Pallas kernels: 136 us -> 128 us
    pallas_call x3, Pallas kernels: 118 us -> 108 us  [the longest x1 47.9 us: finish(): pl.pallas_call(functools.partial(finish_kernel, caps), in_specs=[smem, sm...]
    pallas_call x1, Pallas kernels: 18.1 us -> 20.2 us  [attention(): pl.pallas_call(attention_kernel, grid=(8,), in_specs=[pl.BlockSpec((keys,...]
where the time goes in v4:
time: 139 us
  Pallas kernels  128 us (92%)
  other arithmetic  4.87 us (4%)
  local copies, waits for them, and re-layouts  2.63 us (2%)
  between operations  2.24 us (2%)
    pallas_call x1, Pallas kernels, finish(): pl.pallas_call(functools.partial(finish_kernel, caps), in_specs=[smem, sm...  47.9 us
    pallas_call x1, Pallas kernels, gather(): pl.pallas_call(functools.partial(gather_kernel, caps), in_specs=[pl.Block...  37.6 us
    pallas_call x1, Pallas kernels, spread(): pl.pallas_call(spread_kernel, in_specs=[pl.BlockSpec(memory_space=pltpu.S...  22.6 us
    pallas_call x1, Pallas kernels, attention(): pl.pallas_call(attention_kernel, grid=(8,), in_specs=[pl.BlockSpec((keys,...  20.2 us

profile of v4, /device:TPU:1, one launch (start us, length us, event | category | flops | bytes accessed | tf_op | source)
XLA Modules:
  0.0 138.9 jit_solution(6731752426606787727)
XLA Ops:
  0.6 0.0 copy-start.2
  0.6 0.0 copy-start.3
  0.7 0.0 copy-start
  0.8 22.6 %shard_map.94 = (bf16[8,8,16,256]{3,2,1,0:T(8,128)(2,1)S(1)}, s32[4,2,128]{2,1,0:T(2,128)}) custom-call(s32[1,2,2]{2,1,0:T(2,128)} %mine_ref.1, bf16[8,128,512]{2,1,0:T(8,128)(2,1)} %bitcast.151), custom_call_target="tpu_custom_call" | custom-call | tf_op jit(solution)/shard_map/pallas_call | solution.py:345
  23.4 0.7 multiply_add_fusion
  24.1 0.1 fusion.44
  24.2 0.1 select_reduce_fusion.9
  24.3 0.1 broadcast_compare_fusion
  24.4 0.1 slice_bitcast_fusion.19
  24.5 0.5 fusion.19
  25.0 0.1 reshape.535
  25.2 0.7 convert_reduce_fusion.1
  25.9 0.2 reduce_max.9
  26.1 0.0 copy-done.2
  26.1 0.0 copy-done.3
  26.1 0.6 compare_reduce_fusion
  28.0 0.2 convert_reduce_fusion
  28.3 0.1 convert_element_type.24
  28.4 0.2 convolution_convert_fusion
  28.6 0.2 iota_compare_fusion.4
  28.8 0.0 copy-done
  28.8 38.9 %conditional.2 = (bf16[512,512]{1,0:T(8,128)(2,1)S(1)}) conditional(s32[]{:T(128)} %clamp.4, (pred[2,8,64,64]{3,2,1,0:T(8,128)(4,1)S(1)}, s32[2,64,64]{2,1,0:T(8,128)S(1)}, s32[32]{0:T(128)S(1)}, s32[32]{0:T(128)S(1)}, pred[32]{0:T(512)(128)(4,1)S(1)}, /*index=5*/s32[2,32]{1,0:T(2,128)S(1)}, bf16[8,8,16,256]{3,2,1,0:T(8,128)(2,1)S(1)}, ...), branch_computations={%region_5.7_spmd, %region_7.9_spmd, %region_9.11_spmd} | conditional | flops 16800 | bytes 83112 | solution.py:888
  28.8 0.6 select_reduce_fusion.order_ref
  29.4 0.5 compare_select_fusion.3.loc_ref
  29.9 37.6 %branch_0_fun.4 = bf16[4,128,512]{2,1,0:T(8,128)(2,1)S(1)} custom-call(s32[2,64]{1,0:T(2,128)} %select_reduce_fusion.order_ref, s32[32]{0:T(128)} %compare_select_fusion.3.loc_ref, bf16[8,8,16,256]{3,2,1,0:T(8,128)(2,1)S(1)} %get-tuple-element.495.pool_ref, bf16[8,128,512]{2,1,0:T(8,128)(2,1)S(1)} %get-tuple-element.496.enc_ref), custom_call_target="tpu_custom_call" | custom-call | tf_op jit(solution)/shard_map/cond/branch_0_fun/pallas_call | solution.py:516
  67.8 0.2 and_convert_fusion
  68.0 20.2 %shard_map.95 = (bf16[128,2048]{1,0:T(8,128)(2,1)}, bf16[512,512]{1,0:T(8,128)(2,1)S(1)}, bf16[3,4,2,8,16,256]{5,4,3,2,1,0:T(8,128)(2,1)S(1)}) custom-call(bf16[512,512]{1,0:T(8,128)(2,1)S(1)} %get-tuple-element.685.states_ref, bf16[2,512,2048]{2,1,0:T(8,128)(2,1)} %w_ref.1, bf16[128,2048]{1,0:T(8,128)(2,1)} %bitcast.172, bf16[128,2048]{1,0:T(8,128)(2,1)} %bitcast.173), custom_call_target="tpu_custom_call" | custom-call | flops 7200000000 | bytes 12000000 | tf_op jit(solution)/shard_map/pallas_call | solution.py:231
  88.2 0.0 copy-start.1
  88.2 48.4 %conditional.3 = (f32[2,16,256]{2,1,0:T(8,128)S(1)}, bf16[1,8,128,512]{3,2,1,0:T(8,128)(2,1)S(1)}) conditional(s32[]{:T(128)} %clamp.4, (pred[32,32]{1,0:T(8,128)(4,1)S(1)}, s32[32,32,32]{2,1,0:T(8,128)S(1)}, s32[4,32,32]{2,1,0:T(8,128)S(1)}, s32[32]{0:T(128)S(1)}, s32[2,4,64,1]{2,1,3,0:T(4,128)S(1)}, ...), branch_computations={%region_12.16_spmd, %region_16.20_spmd, %region_20.24_spmd} | conditional | flops 114912 | bytes 207252 | solution.py:897
  88.3 0.1 select_reduce_fusion.3
  88.4 0.1 reduce_sum.99
  88.5 0.1 select_reduce_fusion.4
  88.6 47.9 %branch_0_fun.5 = (bf16[8,128,512]{2,1,0:T(8,128)(2,1)S(1)}, f32[2,16,256]{2,1,0:T(8,128)S(1)}) custom-call(s32[4,32]{1,0:T(4,128)S(1)} %broadcast_add_fusion.2.mate_ref, s32[2,4,64]{2,1,0:T(4,128)S(1)} %broadcast_add_fusion.1.con_ref, s32[3,64]{1,0:T(4,128)S(1)} %pad_add_fusion.fin_ref, bf16[4,128,512]{2,1,0:T(8,128)(2,1)S(1)} %bitcast.155, ...), custom_call_target="tpu_custom_call" | custom-call | tf_op jit(solution)/shard_map/cond/branch_0_fun/pallas_call | solution.py:755
  136.6 0.0 copy-done.1
  136.6 0.8 copy.55
  137.4 1.0 copy.56
  138.3 0.6 copy.57
  (28 shorter events, 0.3 us)
Async XLA Ops:
  0.6 25.4 %copy-start.2 = (s32[4]{0:T(128)S(1)}, s32[4]{0:T(128)}, u32[]{:S(2)}) copy-start(s32[4]{0:T(128)} %constant.320.clone) | copy-start | bytes 52
  0.6 25.4 %copy-start.3 = (s32[4]{0:T(128)S(1)}, s32[4]{0:T(128)}, u32[]{:S(2)}) copy-start(s32[4]{0:T(128)} %constant.319.clone) | copy-start | bytes 52
  0.7 28.1 %copy-start = (bf16[1,8,128,512]{3,2,1,0:T(8,128)(2,1)S(1)}, bf16[1,8,128,512]{3,2,1,0:T(8,128)(2,1)}, u32[]{:S(2)}) copy-start(bf16[1,8,128,512]{3,2,1,0:T(8,128)(2,1)} %param.15) | copy-start | bytes 3145732
  88.2 48.4 %copy-start.1 = (bf16[128,2048]{1,0:T(8,128)(2,1)S(1)}, bf16[128,2048]{1,0:T(8,128)(2,1)}, u32[]{:S(2)}) copy-start(bf16[128,2048]{1,0:T(8,128)(2,1)} %get-tuple-element.564) | copy-start | bytes 1572868

commit v5 on v4

--- a/solution.py
+++ b/solution.py
@@ -93,6 +93,7 @@
     blank = jnp.zeros((64, DH), BF)
     gk_parts = []
     gv_parts = []
+    ahead = []
     for span in range(2):
         q = q_ref[span * 64 : span * 64 + 64, :]
         go = go_ref[span * 64 : span * 64 + 64, :]
@@ -113,13 +114,18 @@
             axis=0,
         )
         scores = lax.dot_general(key, qd, NT, preferred_element_type=F32) * scale
+        gp = lax.dot_general(value, gd, NT, preferred_element_type=F32)
+        ahead.append((key, qd, gd, scores, gp))
+    middle = []
+    for key, qd, gd, scores, gp in ahead:
         top = jnp.max(scores, axis=0, keepdims=True)
         expo = jnp.exp(scores - top)
         weights = expo / jnp.sum(expo, axis=0, keepdims=True)
         weights_b = weights.astype(BF)
-        gp = lax.dot_general(value, gd, NT, preferred_element_type=F32)
         delta = jnp.sum(weights_b.astype(F32) * gp, axis=0, keepdims=True)
         gs = (weights * (gp - delta) * scale).astype(BF)
+        middle.append((key, qd, gd, weights_b, gs))
+    for span, (key, qd, gd, weights_b, gs) in enumerate(middle):
         gv_parts.append(jnp.dot(weights_b, gd, preferred_element_type=F32).astype(BF))
         gk_parts.append(jnp.dot(gs, qd, preferred_element_type=F32).astype(BF))
         gq = lax.dot_general(gs, key, TN, preferred_element_type=F32).astype(BF)
@@ -268,23 +274,29 @@
 
 OUT = ((0, 256), (256, 128), (384, 128))
 BACK = ((0, 128), (128, 256), (384, 128))
+EARLY = 2
 
 
 def piece(member):
     return pl.ds(pl.multiple_of(member * 16, 16), 16)
 
 
-def spread_kernel(
-    mine_ref, enc_ref, pool_ref, packed_ref, ids_ref, team_sem, xy_sem, zc_sem, own_sem
-):
+def spread_kernel(mine_ref, enc_ref, *rest):
+    pool_refs = rest[:EARLY]
+    packed_ref, ids_ref, team_sem, xy_sem, zc_sem, own_sem = rest[EARLY:]
     z, x, y, core = place()
     me = x * 2 + core
-    columns = pl.ds(*OUT[0])
     team = [teammate(z, y, (me + k) % 8) for k in range(1, 8)]
     flat = [at(z, x + k // 4, y + k % 4, core) for k in range(1, 16)]
     upright = [at(z + k // 2, x, y, (core + k % 2) % 2) for k in range(1, 16)]
-    own = pltpu.make_async_copy(enc_ref.at[:, piece(me), columns], pool_ref.at[me], own_sem)
-    own.start()
+    owns = []
+    for h in range(EARLY):
+        owns.append(
+            pltpu.make_async_copy(
+                enc_ref.at[:, piece(me), pl.ds(*OUT[h])], pool_refs[h].at[me], own_sem.at[h]
+            )
+        )
+        owns[h].start()
     lane = lax.broadcasted_iota(jnp.int32, (1, 128), 1) - (z % 4 * 32 + me * 4)
     line = jnp.zeros((1, 128), jnp.int32)
     for ref in range(4):
@@ -303,16 +315,20 @@
             )
         )
     pieces = []
-    for k in range(1, 8):
-        pieces.append(
-            push(
-                enc_ref.at[:, piece((me + k) % 8), columns],
-                pool_ref.at[me],
-                team_sem.at[0, k - 1],
-                team_sem.at[1, k - 1],
-                team[k - 1],
-            )
-        )
+
+    def hand(h):
+        for k in range(1, 8):
+            pieces.append(
+                push(
+                    enc_ref.at[:, piece((me + k) % 8), pl.ds(*OUT[h])],
+                    pool_refs[h].at[me],
+                    team_sem.at[0, h, k - 1],
+                    team_sem.at[1, h, k - 1],
+                    team[k - 1],
+                )
+            )
+
+    hand(0)
     for copy in rows:
         copy.wait_recv()
     planes = []
@@ -326,7 +342,10 @@
                 upright[k - 1],
             )
         )
-    own.wait()
+    for h in range(1, EARLY):
+        hand(h)
+    for copy in owns:
+        copy.wait()
     for copy in planes + pieces:
         copy.wait_recv()
     for yy in range(4):
@@ -348,20 +367,15 @@
             pl.BlockSpec(memory_space=pltpu.SMEM),
             pl.BlockSpec(memory_space=pl.ANY),
         ],
-        out_specs=[
-            pl.BlockSpec(memory_space=pltpu.VMEM),
-            pl.BlockSpec(memory_space=pltpu.VMEM),
-        ],
-        out_shape=[
-            jax.ShapeDtypeStruct((8, 8, 16, OUT[0][1]), BF),
-            jax.ShapeDtypeStruct((4, 2, 128), jnp.int32),
-        ],
+        out_specs=[pl.BlockSpec(memory_space=pltpu.VMEM)] * (EARLY + 1),
+        out_shape=[jax.ShapeDtypeStruct((8, 8, 16, wide), BF) for _, wide in OUT[:EARLY]]
+        + [jax.ShapeDtypeStruct((4, 2, 128), jnp.int32)],
         scratch_shapes=[
             pltpu.VMEM((8, 2, 4, 4, 1, 128), jnp.int32),
-            pltpu.SemaphoreType.DMA((2, 7)),
+            pltpu.SemaphoreType.DMA((2, EARLY, 7)),
             pltpu.SemaphoreType.DMA((2, 15)),
             pltpu.SemaphoreType.DMA((2, 15)),
-            pltpu.SemaphoreType.DMA,
+            pltpu.SemaphoreType.DMA((EARLY,)),
         ],
         compiler_params=pltpu.CompilerParams(
             collective_id=1, has_side_effects=True, vmem_limit_bytes=60 * 2**20
@@ -378,13 +392,14 @@
     return list(zip([0] + ends[:-1], ends))
 
 
-def gather_kernel(caps, order_ref, loc_ref, pool_ref, enc_ref, states_ref, *scratch):
+def gather_kernel(caps, order_ref, loc_ref, *rest):
     count = len(OUT)
-    pools = (pool_ref,) + scratch[: count - 1]
-    packeds = scratch[count - 1 : 2 * count - 1]
-    arrs = scratch[2 * count - 1 : 3 * count - 1]
-    stages = scratch[3 * count - 1 : 4 * count - 1]
-    ring_sem, team_sem, spread_sem, own_sem = scratch[4 * count - 1 :]
+    late = count - EARLY
+    enc_ref, states_ref = rest[EARLY : EARLY + 2]
+    pools = rest[:EARLY] + rest[EARLY + 2 : EARLY + 2 + late]
+    scratch = rest[EARLY + 2 + late :]
+    packeds, arrs, stages = (scratch[k * count : k * count + count] for k in range(3))
+    ring_sem, team_sem, spread_sem, own_sem = scratch[3 * count :]
     z, x, y, core = place()
     me = x * 2 + core
     total = sum(caps)
@@ -394,10 +409,10 @@
     ahead = at(z + 1, x, y, core)
     behind = at(z - 1, x, y, core)
     owns = []
-    for h in range(1, count):
+    for h in range(EARLY, count):
         owns.append(
             pltpu.make_async_copy(
-                enc_ref.at[:, piece(me), pl.ds(*OUT[h])], pools[h].at[me], own_sem.at[h - 1]
+                enc_ref.at[:, piece(me), pl.ds(*OUT[h])], pools[h].at[me], own_sem.at[h - EARLY]
             )
         )
         owns[-1].start()
@@ -475,18 +490,20 @@
             pieces[h, k] = push(
                 enc_ref.at[:, piece((me + k) % 8), pl.ds(*OUT[h])],
                 pools[h].at[me],
-                spread_sem.at[0, h - 1, k - 1],
-                spread_sem.at[1, h - 1, k - 1],
+                spread_sem.at[0, h - EARLY, k - 1],
+                spread_sem.at[1, h - EARLY, k - 1],
                 friends[k - 1],
             )
 
     def here(h):
-        owns[h - 1].wait()
+        if h < EARLY:
+            return
+        owns[h - EARLY].wait()
         for k in range(1, 8):
             pieces[h, k].wait_recv()
 
-    more(1)
-    more(2)
+    for h in range(EARLY, count):
+        more(h)
     first_hop(0)
     here(1)
     first_hop(1)
@@ -510,33 +527,30 @@
         copy.wait_send()
 
 
-def gather(caps, number, order, loc, pool, enc):
+def gather(caps, number, order, loc, pools, enc):
     total = sum(caps)
     count = len(OUT)
     return pl.pallas_call(
         functools.partial(gather_kernel, caps),
-        in_specs=[
-            pl.BlockSpec(memory_space=pltpu.SMEM),
-            pl.BlockSpec(memory_space=pltpu.SMEM),
-            pl.BlockSpec(memory_space=pltpu.VMEM),
-            pl.BlockSpec(memory_space=pl.ANY),
-        ],
+        in_specs=[pl.BlockSpec(memory_space=pltpu.SMEM)] * 2
+        + [pl.BlockSpec(memory_space=pltpu.VMEM)] * EARLY
+        + [pl.BlockSpec(memory_space=pl.ANY)],
         out_specs=pl.BlockSpec(memory_space=pltpu.VMEM),
         out_shape=jax.ShapeDtypeStruct((4, 128, 512), BF),
-        scratch_shapes=[pltpu.VMEM((8, 8, 16, wide), BF) for _, wide in OUT[1:]]
+        scratch_shapes=[pltpu.VMEM((8, 8, 16, wide), BF) for _, wide in OUT[EARLY:]]
         + [pltpu.VMEM((2, caps[0], 16, wide), BF) for _, wide in OUT]
         + [pltpu.VMEM((2 * total + 64, 16, wide), BF) for _, wide in OUT]
         + [pltpu.VMEM((8, 4, 16, wide), BF) for _, wide in OUT]
         + [
             pltpu.SemaphoreType.DMA((2, count, 2, 4, 4)),
             pltpu.SemaphoreType.DMA((2, count, 7)),
-            pltpu.SemaphoreType.DMA((2, count - 1, 7)),
-            pltpu.SemaphoreType.DMA((count - 1,)),
+            pltpu.SemaphoreType.DMA((2, count - EARLY, 7)),
+            pltpu.SemaphoreType.DMA((count - EARLY,)),
         ],
         compiler_params=pltpu.CompilerParams(
             collective_id=number, has_side_effects=True, vmem_limit_bytes=60 * 2**20
         ),
-    )(order, loc, pool, enc)
+    )(order, loc, *pools, enc)
 
 
 def finish_kernel(
@@ -883,12 +897,12 @@
 
 def body(queries, grad_out, enc_states, neighbour_ids, kv_weight):
     enc = enc_states[0]
-    pool, ids = spread(neighbour_ids, enc)
+    *pools, ids = spread(neighbour_ids, enc)
     level, order, mate, con, locate, collect = plan(ids.reshape(4, 256))
     states = lax.switch(
         level,
         [
-            lambda caps=caps, number=number: gather(caps, number, order, locate(caps), pool, enc)
+            lambda caps=caps, number=number: gather(caps, number, order, locate(caps), pools, enc)
             for caps, number in zip(CAPS, (2, 3, 7))
         ],
     )

time: 139 us -> 136 us (0.978)
  Pallas kernels: 128 us -> 125 us
    pallas_call x1, Pallas kernels: 37.6 us -> 34.9 us  [gather(): pl.pallas_call(functools.partial(gather_kernel, caps), in_specs=[pl.Block...]
    pallas_call x1, Pallas kernels: 20.2 us -> 18.4 us  [attention(): pl.pallas_call(attention_kernel, grid=(8,), in_specs=[pl.BlockSpec((keys,...]
where the time goes in v5:
time: 136 us
  Pallas kernels  125 us (92%)
  other arithmetic  4.87 us (4%)
  local copies, waits for them, and re-layouts  2.63 us (2%)
  between operations  2.24 us (2%)
    pallas_call x1, Pallas kernels, finish(): pl.pallas_call(functools.partial(finish_kernel, caps), in_specs=[smem, sm...  48 us
    pallas_call x1, Pallas kernels, gather(): pl.pallas_call(functools.partial(gather_kernel, caps), in_specs=[pl.Block...  34.9 us
    pallas_call x1, Pallas kernels, spread(): pl.pallas_call(spread_kernel, in_specs=[pl.BlockSpec(memory_space=pltpu.S...  23.6 us
    pallas_call x1, Pallas kernels, attention(): pl.pallas_call(attention_kernel, grid=(8,), in_specs=[pl.BlockSpec((keys,...  18.4 us

profile of v5, /device:TPU:1, one launch (start us, length us, event | category | flops | bytes accessed | tf_op | source)
XLA Modules:
  0.0 135.5 jit_solution(4963635103908308352)
XLA Ops:
  0.6 0.0 copy-start.2
  0.6 0.0 copy-start.3
  0.7 0.0 copy-start
  0.8 23.6 %shard_map.94 = (bf16[8,8,16,256]{3,2,1,0:T(8,128)(2,1)S(1)}, bf16[8,8,16,128]{3,2,1,0:T(8,128)(2,1)S(1)}, s32[4,2,128]{2,1,0:T(2,128)}) custom-call(s32[1,2,2]{2,1,0:T(2,128)} %mine_ref.1, bf16[8,128,512]{2,1,0:T(8,128)(2,1)} %bitcast.151), custom_call_target="tpu_custom_call" | custom-call | tf_op jit(solution)/shard_map/pallas_call | solution.py:364
  24.4 0.7 multiply_add_fusion
  25.1 0.1 fusion.44
  25.2 0.1 select_reduce_fusion.9
  25.3 0.1 broadcast_compare_fusion
  25.4 0.1 slice_bitcast_fusion.19
  25.5 0.5 fusion.19
  25.9 0.1 reshape.535
  26.1 0.7 convert_reduce_fusion.1
  26.8 0.2 reduce_max.9
  27.0 0.0 copy-done.2
  27.0 0.0 copy-done.3
  27.0 0.6 compare_reduce_fusion
  29.0 0.2 convert_reduce_fusion
  29.2 0.1 convert_element_type.24
  29.3 0.2 convolution_convert_fusion
  29.5 0.2 iota_compare_fusion.4
  29.7 0.0 copy-done
  29.7 36.1 %conditional.2 = (bf16[512,512]{1,0:T(8,128)(2,1)S(1)}) conditional(s32[]{:T(128)} %clamp.4, (pred[2,8,64,64]{3,2,1,0:T(8,128)(4,1)S(1)}, s32[2,64,64]{2,1,0:T(8,128)S(1)}, s32[32]{0:T(128)S(1)}, s32[32]{0:T(128)S(1)}, pred[32]{0:T(512)(128)(4,1)S(1)}, /*index=5*/s32[2,32]{1,0:T(2,128)S(1)}, bf16[8,8,16,256]{3,2,1,0:T(8,128)(2,1)S(1)}, ...), branch_computations={%region_5.7_spmd, %region_7.9_spmd, %region_9.11_spmd} | conditional | flops 16800 | bytes 83112 | solution.py:902
  29.8 0.6 select_reduce_fusion.order_ref
  30.3 0.5 compare_select_fusion.3.loc_ref
  30.9 34.9 %branch_0_fun.4 = bf16[4,128,512]{2,1,0:T(8,128)(2,1)S(1)} custom-call(s32[2,64]{1,0:T(2,128)} %select_reduce_fusion.order_ref, s32[32]{0:T(128)} %compare_select_fusion.3.loc_ref, bf16[8,8,16,256]{3,2,1,0:T(8,128)(2,1)S(1)} %get-tuple-element.504.rest_0_, bf16[8,8,16,128]{3,2,1,0:T(8,128)(2,1)S(1)} %get-tuple-element.505.rest_1_, ...), custom_call_target="tpu_custom_call" | custom-call | tf_op jit(solution)/shard_map/cond/branch_0_fun/pallas_call | solution.py:533
  66.0 0.2 and_convert_fusion
  66.2 18.4 %shard_map.95 = (bf16[128,2048]{1,0:T(8,128)(2,1)}, bf16[512,512]{1,0:T(8,128)(2,1)S(1)}, bf16[3,4,2,8,16,256]{5,4,3,2,1,0:T(8,128)(2,1)S(1)}) custom-call(bf16[512,512]{1,0:T(8,128)(2,1)S(1)} %get-tuple-element.699.states_ref, bf16[2,512,2048]{2,1,0:T(8,128)(2,1)} %w_ref.1, bf16[128,2048]{1,0:T(8,128)(2,1)} %bitcast.172, bf16[128,2048]{1,0:T(8,128)(2,1)} %bitcast.173), custom_call_target="tpu_custom_call" | custom-call | flops 7200000000 | bytes 12000000 | tf_op jit(solution)/shard_map/pallas_call | solution.py:237
  84.5 0.0 copy-start.1
  84.5 48.6 %conditional.3 = (f32[2,16,256]{2,1,0:T(8,128)S(1)}, bf16[1,8,128,512]{3,2,1,0:T(8,128)(2,1)S(1)}) conditional(s32[]{:T(128)} %clamp.4, (pred[32,32]{1,0:T(8,128)(4,1)S(1)}, s32[32,32,32]{2,1,0:T(8,128)S(1)}, s32[4,32,32]{2,1,0:T(8,128)S(1)}, s32[32]{0:T(128)S(1)}, s32[2,4,64,1]{2,1,3,0:T(4,128)S(1)}, ...), branch_computations={%region_12.16_spmd, %region_16.20_spmd, %region_20.24_spmd} | conditional | flops 114912 | bytes 207252 | solution.py:911
  84.8 0.1 select_reduce_fusion.3
  85.0 0.1 reduce_sum.99
  85.0 0.1 select_reduce_fusion.4
  85.1 48.0 %branch_0_fun.5 = (bf16[8,128,512]{2,1,0:T(8,128)(2,1)S(1)}, f32[2,16,256]{2,1,0:T(8,128)S(1)}) custom-call(s32[4,32]{1,0:T(4,128)S(1)} %broadcast_add_fusion.2.mate_ref, s32[2,4,64]{2,1,0:T(4,128)S(1)} %broadcast_add_fusion.1.con_ref, s32[3,64]{1,0:T(4,128)S(1)} %pad_add_fusion.fin_ref, bf16[4,128,512]{2,1,0:T(8,128)(2,1)S(1)} %bitcast.155, ...), custom_call_target="tpu_custom_call" | custom-call | tf_op jit(solution)/shard_map/cond/branch_0_fun/pallas_call | solution.py:769
  133.1 0.0 copy-done.1
  133.1 0.8 copy.55
  133.9 1.0 copy.56
  134.9 0.6 copy.57
  (28 shorter events, 0.3 us)
Async XLA Ops:
  0.6 26.4 %copy-start.2 = (s32[4]{0:T(128)S(1)}, s32[4]{0:T(128)}, u32[]{:S(2)}) copy-start(s32[4]{0:T(128)} %constant.320.clone) | copy-start | bytes 52
  0.6 26.4 %copy-start.3 = (s32[4]{0:T(128)S(1)}, s32[4]{0:T(128)}, u32[]{:S(2)}) copy-start(s32[4]{0:T(128)} %constant.319.clone) | copy-start | bytes 52
  0.7 29.1 %copy-start = (bf16[1,8,128,512]{3,2,1,0:T(8,128)(2,1)S(1)}, bf16[1,8,128,512]{3,2,1,0:T(8,128)(2,1)}, u32[]{:S(2)}) copy-start(bf16[1,8,128,512]{3,2,1,0:T(8,128)(2,1)} %param.15) | copy-start | bytes 3145732
  84.5 48.6 %copy-start.1 = (bf16[128,2048]{1,0:T(8,128)(2,1)S(1)}, bf16[128,2048]{1,0:T(8,128)(2,1)}, u32[]{:S(2)}) copy-start(bf16[128,2048]{1,0:T(8,128)(2,1)} %get-tuple-element.578) | copy-start | bytes 1572868

commit v6 on v5

--- a/solution.py
+++ b/solution.py
@@ -57,6 +57,7 @@
 def attention_kernel(
     states_ref,
     w_ref,
+    next_ref,
     q_ref,
     go_ref,
     gq_ref,
@@ -64,6 +65,8 @@
     sums_ref,
     st_ref,
     acc_ref,
+    now_ref,
+    later_ref,
     pair_out,
     pair_in,
     far_out,
@@ -81,6 +84,10 @@
     def _():
         st_ref[...] = states_ref[...].T
         acc_ref[...] = jnp.zeros_like(acc_ref)
+        for kind in range(2):
+            later_ref[kind] = jnp.dot(
+                states_ref[...], w_ref[kind], preferred_element_type=F32
+            ).astype(BF)
         barrier = pltpu.get_barrier_semaphore()
         for friend in [other] + sides:
             pl.semaphore_signal(barrier, inc=1, device_id=friend, device_id_type=MESH)
@@ -88,8 +95,9 @@
     states = states_ref[...]
     wk = w_ref[0]
     wv = w_ref[1]
-    keys = jnp.dot(states, wk, preferred_element_type=F32).astype(BF)
-    values = jnp.dot(states, wv, preferred_element_type=F32).astype(BF)
+    now_ref[...] = later_ref[...]
+    keys = now_ref[0]
+    values = now_ref[1]
     blank = jnp.zeros((64, DH), BF)
     gk_parts = []
     gv_parts = []
@@ -117,6 +125,8 @@
         gp = lax.dot_general(value, gd, NT, preferred_element_type=F32)
         ahead.append((key, qd, gd, scores, gp))
     middle = []
+    for kind in range(2):
+        later_ref[kind] = jnp.dot(states, next_ref[kind], preferred_element_type=F32).astype(BF)
     for key, qd, gd, scores, gp in ahead:
         top = jnp.max(scores, axis=0, keepdims=True)
         expo = jnp.exp(scores - top)
@@ -134,8 +144,12 @@
     gk = jnp.concatenate(gk_parts, axis=0)
     gv = jnp.concatenate(gv_parts, axis=0)
     total = acc_ref[...]
-    total = total + lax.dot_general(gk, wk, NT, preferred_element_type=F32)
-    total = total + lax.dot_general(gv, wv, NT, preferred_element_type=F32)
+    total = total + lax.dot_general(
+        jnp.concatenate([gk, gv], axis=1),
+        jnp.concatenate([wk, wv], axis=1),
+        NT,
+        preferred_element_type=F32,
+    )
     acc_ref[...] = total
 
     @pl.when(step == pl.num_programs(0) - 1)
@@ -240,6 +254,7 @@
         in_specs=[
             pl.BlockSpec((keys, enc), lambda i: (0, 0)),
             pl.BlockSpec((2, enc, 256), lambda i: (0, 0, columns(i))),
+            pl.BlockSpec((2, enc, 256), lambda i: (0, 0, columns((i + 1) % 8))),
             pl.BlockSpec((tokens, 256), lambda i: (0, columns(i))),
             pl.BlockSpec((tokens, 256), lambda i: (0, columns(i))),
         ],
@@ -256,6 +271,8 @@
         scratch_shapes=[
             pltpu.VMEM((enc, keys), BF),
             pltpu.VMEM((keys, enc), F32),
+            pltpu.VMEM((2, keys, 256), BF),
+            pltpu.VMEM((2, keys, 256), BF),
             pltpu.VMEM((4, 4, 2, 8, 16, 256), BF),
             pltpu.VMEM((4, 4, 2, 8, 16, 256), BF),
             pltpu.VMEM((4, 2, 8, 16, 256), BF),
@@ -269,7 +286,7 @@
         cost_estimate=pl.CostEstimate(
             flops=7_200_000_000, bytes_accessed=12_000_000, transcendentals=600_000
         ),
-    )(states, weights, queries, grad_out)
+    )(states, weights, weights, queries, grad_out)
 
 
 OUT = ((0, 256), (256, 128), (384, 128))

time: 136 us -> 137 us (level); the launches traced: 136 us -> 139 us
  Pallas kernels: 125 us -> 129 us
    pallas_call x1, Pallas kernels: 34.9 us -> 37.4 us  [gather(): pl.pallas_call(functools.partial(gather_kernel, caps), in_specs=[pl.Block...]
    pallas_call x1, Pallas kernels: 48 us -> 49.6 us  [finish(): pl.pallas_call(functools.partial(finish_kernel, caps), in_specs=[smem, sm...]
where the time goes in v6:
time: 137 us; the launch traced here: 139 us
  Pallas kernels  129 us (94%)
  other arithmetic  4.87 us (4%)
  local copies, waits for them, and re-layouts  2.63 us (2%)
  between operations  2.24 us (2%)
    pallas_call x1, Pallas kernels, finish(): pl.pallas_call(functools.partial(finish_kernel, caps), in_specs=[smem, sm...  49.6 us
    pallas_call x1, Pallas kernels, gather(): pl.pallas_call(functools.partial(gather_kernel, caps), in_specs=[pl.Block...  37.4 us
    pallas_call x1, Pallas kernels, spread(): pl.pallas_call(spread_kernel, in_specs=[pl.BlockSpec(memory_space=pltpu.S...  23.6 us
    pallas_call x1, Pallas kernels, attention(): pl.pallas_call(attention_kernel, grid=(8,), in_specs=[pl.BlockSpec((keys,...  18.1 us

profile of v6, /device:TPU:1, one launch (start us, length us, event | category | flops | bytes accessed | tf_op | source)
XLA Modules:
  0.0 139.3 jit_solution(2656123794401349339)
XLA Ops:
  0.6 0.0 copy-start.2
  0.6 0.0 copy-start.3
  0.7 0.0 copy-start
  0.8 23.6 %shard_map.94 = (bf16[8,8,16,256]{3,2,1,0:T(8,128)(2,1)S(1)}, bf16[8,8,16,128]{3,2,1,0:T(8,128)(2,1)S(1)}, s32[4,2,128]{2,1,0:T(2,128)}) custom-call(s32[1,2,2]{2,1,0:T(2,128)} %mine_ref.1, bf16[8,128,512]{2,1,0:T(8,128)(2,1)} %bitcast.151), custom_call_target="tpu_custom_call" | custom-call | tf_op jit(solution)/shard_map/pallas_call | solution.py:381
  24.4 0.7 multiply_add_fusion
  25.1 0.1 fusion.44
  25.2 0.1 select_reduce_fusion.9
  25.3 0.1 broadcast_compare_fusion
  25.4 0.1 slice_bitcast_fusion.19
  25.5 0.5 fusion.19
  25.9 0.1 reshape.535
  26.1 0.7 convert_reduce_fusion.1
  26.8 0.2 reduce_max.9
  27.0 0.0 copy-done.2
  27.0 0.0 copy-done.3
  27.0 0.6 compare_reduce_fusion
  29.0 0.2 convert_reduce_fusion
  29.2 0.1 convert_element_type.24
  29.3 0.2 convolution_convert_fusion
  29.5 0.2 iota_compare_fusion.4
  29.7 0.0 copy-done
  29.7 38.5 %conditional.2 = (bf16[512,512]{1,0:T(8,128)(2,1)S(1)}) conditional(s32[]{:T(128)} %clamp.4, (pred[2,8,64,64]{3,2,1,0:T(8,128)(4,1)S(1)}, s32[2,64,64]{2,1,0:T(8,128)S(1)}, s32[32]{0:T(128)S(1)}, s32[32]{0:T(128)S(1)}, pred[32]{0:T(512)(128)(4,1)S(1)}, /*index=5*/s32[2,32]{1,0:T(2,128)S(1)}, bf16[8,8,16,256]{3,2,1,0:T(8,128)(2,1)S(1)}, ...), branch_computations={%region_5.7_spmd, %region_7.9_spmd, %region_9.11_spmd} | conditional | flops 16800 | bytes 83112 | solution.py:919
  29.8 0.6 select_reduce_fusion.1.order_ref
  30.4 0.5 compare_select_fusion.7.loc_ref
  30.9 37.4 %branch_1_fun.4 = bf16[4,128,512]{2,1,0:T(8,128)(2,1)S(1)} custom-call(s32[2,64]{1,0:T(2,128)} %select_reduce_fusion.1.order_ref, s32[32]{0:T(128)} %compare_select_fusion.7.loc_ref, bf16[8,8,16,256]{3,2,1,0:T(8,128)(2,1)S(1)} %get-tuple-element.513.rest_0_, bf16[8,8,16,128]{3,2,1,0:T(8,128)(2,1)S(1)} %get-tuple-element.514.rest_1_, ...), custom_call_target="tpu_custom_call" | custom-call | tf_op jit(solution)/shard_map/cond/branch_1_fun/pallas_call | solution.py:550
  68.4 0.2 and_convert_fusion
  68.6 18.1 %shard_map.95 = (bf16[128,2048]{1,0:T(8,128)(2,1)}, bf16[512,512]{1,0:T(8,128)(2,1)S(1)}, bf16[3,4,2,8,16,256]{5,4,3,2,1,0:T(8,128)(2,1)S(1)}) custom-call(bf16[512,512]{1,0:T(8,128)(2,1)S(1)} %get-tuple-element.699.states_ref, bf16[2,512,2048]{2,1,0:T(8,128)(2,1)} %next_ref.1, bf16[2,512,2048]{2,1,0:T(8,128)(2,1)} %next_ref.1, bf16[128,2048]{1,0:T(8,128)(2,1)} %bitcast.172, ...), custom_call_target="tpu_custom_call" | custom-call | flops 7200000000 | bytes 12000000 | tf_op jit(solution)/shard_map/pallas_call | solution.py:251
  86.7 0.0 copy-start.1
  86.7 50.2 %conditional.3 = (f32[2,16,256]{2,1,0:T(8,128)S(1)}, bf16[1,8,128,512]{3,2,1,0:T(8,128)(2,1)S(1)}) conditional(s32[]{:T(128)} %clamp.4, (pred[32,32]{1,0:T(8,128)(4,1)S(1)}, s32[32,32,32]{2,1,0:T(8,128)S(1)}, s32[4,32,32]{2,1,0:T(8,128)S(1)}, s32[32]{0:T(128)S(1)}, s32[2,4,64,1]{2,1,3,0:T(4,128)S(1)}, ...), branch_computations={%region_12.16_spmd, %region_16.20_spmd, %region_20.24_spmd} | conditional | flops 114912 | bytes 207252 | solution.py:928
  87.0 0.1 select_reduce_fusion.5
  87.2 0.1 reduce_sum.102
  87.2 0.1 select_reduce_fusion.6
  87.3 49.6 %branch_1_fun.5 = (bf16[8,128,512]{2,1,0:T(8,128)(2,1)S(1)}, f32[2,16,256]{2,1,0:T(8,128)S(1)}) custom-call(s32[4,32]{1,0:T(4,128)S(1)} %broadcast_add_fusion.6.mate_ref, s32[2,4,64]{2,1,0:T(4,128)S(1)} %broadcast_add_fusion.5.con_ref, s32[3,64]{1,0:T(4,128)S(1)} %pad_add_fusion.1.fin_ref, bf16[4,128,512]{2,1,0:T(8,128)(2,1)S(1)} %bitcast.156, ...), custom_call_target="tpu_custom_call" | custom-call | tf_op jit(solution)/shard_map/cond/branch_1_fun/pallas_call | solution.py:786
  136.9 0.0 copy-done.1
  136.9 0.8 copy.55
  137.7 1.0 copy.56
  138.7 0.6 copy.57
  (28 shorter events, 0.3 us)
Async XLA Ops:
  0.6 26.4 %copy-start.2 = (s32[4]{0:T(128)S(1)}, s32[4]{0:T(128)}, u32[]{:S(2)}) copy-start(s32[4]{0:T(128)} %constant.320.clone) | copy-start | bytes 52
  0.6 26.4 %copy-start.3 = (s32[4]{0:T(128)S(1)}, s32[4]{0:T(128)}, u32[]{:S(2)}) copy-start(s32[4]{0:T(128)} %constant.319.clone) | copy-start | bytes 52
  0.7 29.1 %copy-start = (bf16[1,8,128,512]{3,2,1,0:T(8,128)(2,1)S(1)}, bf16[1,8,128,512]{3,2,1,0:T(8,128)(2,1)}, u32[]{:S(2)}) copy-start(bf16[1,8,128,512]{3,2,1,0:T(8,128)(2,1)} %param.15) | copy-start | bytes 3145732
  86.7 50.2 %copy-start.1 = (bf16[128,2048]{1,0:T(8,128)(2,1)S(1)}, bf16[128,2048]{1,0:T(8,128)(2,1)}, u32[]{:S(2)}) copy-start(bf16[128,2048]{1,0:T(8,128)(2,1)} %get-tuple-element.578) | copy-start | bytes 1572868
